TPU v7x, 256 devices: a whole 4x4x8 slice. The times are simulated.
256 devices in a mesh: occ: 64 (over z, y, core), vir: 4 (over x).
Axes of the slice: x: 4, y: 4, z: 8, core: 2. Of those that a mesh axis runs over, the one named last changes fastest.
Arguments:
- chol: bfloat16 [2560, 128, 1408], P('occ', None, 'vir'), may hold values from -0.125 to 0.125
- dressed: bfloat16 [2560, 128, 1408], P('occ', None, 'vir'), may hold values from -6 to 6
- pair_mask: int32 [128, 128], replicated, may hold values 0 or 1
- sym_mask: int32 [88, 88], replicated, may hold values 0 or 1
Outputs:
- residual: bfloat16 [128, 2, 1408, 1408], P('occ', None, 'vir')
All inputs are finite; a program needn't handle non-finite values.
Results may differ from a plain program's by a relative error of at most 0.0051.
Values may be sent and summed in bfloat16 or wider, within the bound.
No kernel may reach another device: no remote copies, remote signals or barrier semaphores. Data moves between devices by JAX's collectives and lax.ppermute only.
A program may use at most 128 MiB of HBM per device.

v0:
```python
import jax
import jax.numpy as jnp
from jax import lax
from jax.sharding import PartitionSpec as P

SLAB = 16


def swapped(block, axis, bit):
    count = lax.axis_size(axis)
    route = []
    for low in range(count):
        high = low | 1 << bit
        if high != low and high < count:
            route += [(low, high), (high, low)]
    return lax.ppermute(block, axis, route)


def contract(left, right):
    return jnp.einsum("pia,pjb->ijab", left, right, preferred_element_type=jnp.float32)


def local(chol, dressed, pair_mask, sym_mask):
    count = lax.axis_size("occ")
    top_bit = count.bit_length() - 2
    width = chol.shape[1] // count
    quarter = chol.shape[2]
    own_l, own_x = (
        lax.all_to_all(chol, "occ", split_axis=1, concat_axis=0, tiled=True),
        lax.all_to_all(dressed, "occ", split_axis=1, concat_axis=0, tiled=True),
    )
    far_x = swapped(own_x, "occ", top_bit)
    direct = contract(own_l, lax.all_gather(far_x, "vir", axis=2, tiled=True)).astype(jnp.bfloat16)
    moved = lax.all_to_all(direct, "vir", split_axis=3, concat_axis=2, tiled=True)
    moved = swapped(moved, "occ", top_bit)
    mirrored = jnp.transpose(moved, (1, 0, 3, 2))
    direct, mirrored = lax.optimization_barrier((direct, mirrored))
    block = lax.axis_index("occ")
    mirror = (block + count // 2) % count
    pairs = lax.dynamic_slice(pair_mask, (block * width, mirror * width), (width, width)).astype(
        jnp.float32
    )
    group = lax.axis_index("vir")
    rows_per = quarter // SLAB
    sym_rows = lax.dynamic_slice_in_dim(sym_mask, group * rows_per, rows_per, 0)
    expand = jnp.repeat(jnp.repeat(sym_rows.astype(jnp.float32), SLAB, 0), SLAB, 1)
    total = direct.astype(jnp.float32) + mirrored.astype(jnp.float32)
    return (pairs[:, :, None, None] * expand[None, None] * total).astype(jnp.bfloat16)


def solution(mesh):
    placed = (P("occ", None, "vir"), P("occ", None, "vir"), P(), P())
    return jax.shard_map(
        local, mesh=mesh, in_specs=placed, out_specs=P("occ", None, "vir", None), check_vma=False
    )
```

profile of v0, /device:TPU:8, one launch (start us, length us, event | category | flops | bytes accessed | tf_op | source)
XLA Modules:
  0.0 706.9 jit_solution(15021410068493180126)
XLA Ops:
  6.5 0.0 all-gather.2.cloned.1.call-start
  6.5 6.2 copy.35
  12.8 102.7 %all_to_all.54 = bf16[40,128,352]{2,0,1:T(8,128)(2,1)S(1)} all-to-all(bf16[40,128,352]{2,0,1:T(8,128)(2,1)} %copy.35), channel_id=1, replica_groups=mesh['occ'=64,'vir'=4] {'occ'}, dimensions={1} | all-to-all | bytes 7208960 | tf_op jit(solution)/shard_map/all_to_all | solution.py:30
  115.5 2.3 copy.36
  117.8 6.1 copy.37
  123.8 0.4 collective-permute-start
  124.2 101.8 %collective-permute-done = bf16[2560,2,352]{0,2,1:T(8,128)(2,1)} collective-permute-done((bf16[2560,2,352]{0,2,1:T(8,128)(2,1)}, bf16[2560,2,352]{0,2,1:T(8,128)(2,1)}, u32[]{:S(2)}, u32[]{:S(2)}) %collective-permute-start) | collective-permute-done | bytes 3604512 | tf_op jit(solution)/shard_map/ppermute | solution.py:16
  226.0 0.0 all-gather.2.cloned.1.call-update
  226.1 6.2 copy.38
  232.3 155.2 %all_to_all.55 = bf16[40,128,352]{2,0,1:T(8,128)(2,1)S(1)} all-to-all(bf16[40,128,352]{2,0,1:T(8,128)(2,1)} %copy.38), channel_id=1, replica_groups=mesh['occ'=64,'vir'=4] {'occ'}, dimensions={1} | all-to-all | bytes 7208960 | tf_op jit(solution)/shard_map/all_to_all | solution.py:29
  387.5 2.3 copy.39
  389.8 28.5 %all-gather.2.cloned.1.call-done = bf16[2560,2,1408]{0,2,1:T(8,128)(2,1)} async-done(((bf16[2560,2,352]{0,2,1:T(8,128)(2,1)}), bf16[2560,2,1408]{0,2,1:T(8,128)(2,1)}) %all-gather.2.cloned.1.call-update) | async-done | bytes 14417936 | tf_op jit(solution)/shard_map/all_gather | solution.py:33
  418.3 17.1 %fusion.5 = bf16[2,2,352,1408]{3,2,0,1:T(8,128)(2,1)} fusion(bf16[2560,2,352,1]{2,0,1,3:T(8,128)(2,1)} %bitcast.37, bf16[2560,2,1408]{0,2,1:T(8,128)(2,1)} %all-gather.2.cloned.1.call-done), kind=kOutput, calls=%fused_computation.5 | convolution fusion | flops 10152198144 | bytes 21987328 | tf_op jit(solution)/shard_map/pia,pjb->ijab/dot_general | solution.py:20
  435.4 12.4 %copy.41 = bf16[2,2,352,1408]{2,0,1,3:T(2,128)(2,1)} copy(bf16[2,2,352,1408]{3,2,0,1:T(8,128)(2,1)} %fusion.5) | data formatting | bytes 7929856 | tf_op jit(solution)/shard_map/convert_element_type | solution.py:33
  447.7 54.3 %all_to_all.56 = bf16[2,2,352,1408]{2,0,1,3:T(2,128)(2,1)S(1)} all-to-all(bf16[2,2,352,1408]{2,0,1,3:T(2,128)(2,1)} %copy.41), channel_id=1, replica_groups=mesh['occ'=64,'vir'=4] {'vir'}, dimensions={3} | all-to-all | bytes 7929856 | tf_op jit(solution)/shard_map/all_to_all | solution.py:34
  502.0 5.3 copy.48
  507.3 8.1 %all_to_all.50 = bf16[2,2,1408,352]{2,3,1,0:T(8,128)(2,1)} reshape(bf16[2,2,4,352,352]{3,2,4,1,0:T(4,128)(2,1)} %bitcast.32) | data formatting | bytes 7929856 | tf_op jit(solution)/shard_map/all_to_all | solution.py:34
  515.4 5.7 collective-permute-start.1
  521.1 0.7 dynamic-slice_convert_fusion
  521.9 0.1 copy.33
  522.0 0.1 broadcast_in_dim.8
  522.1 2.0 copy.34
  524.2 0.8 dynamic-slice_convert_fusion.1
  524.9 0.1 copy.32
  525.0 167.5 %collective-permute-done.1 = bf16[2,2,1408,352]{2,3,1,0:T(8,128)(2,1)} collective-permute-done((bf16[2,2,1408,352]{2,3,1,0:T(8,128)(2,1)}, bf16[2,2,1408,352]{2,3,1,0:T(8,128)(2,1)}, u32[]{:S(2)}, u32[]{:S(2)}) %collective-permute-start.1) | collective-permute-done | bytes 3964960 | tf_op jit(solution)/shard_map/ppermute | solution.py:16
  692.5 5.4 multiply_convert_fusion
  697.9 2.2 copy.43
  (1 shorter events, 0.0 us)
Async XLA Ops:
  6.5 411.8 %all-gather.2.cloned.1.call-start = ((), (), s32[]{:S(2)}) async-start(), calls=%async_computation.3 | async-start | bytes 18022400 | tf_op jit(solution)/shard_map/all_gather | solution.py:33
  123.8 102.2 %collective-permute-start = (bf16[2560,2,352]{0,2,1:T(8,128)(2,1)}, bf16[2560,2,352]{0,2,1:T(8,128)(2,1)}, u32[]{:S(2)}, u32[]{:S(2)}) collective-permute-start(bf16[2560,2,352]{0,2,1:T(8,128)(2,1)} %copy.37), channel_id=1, source_target_pairs={{0,128},{128,0},{4,132},{132,4},{8,136},{136,8},{12,140},{140,12},... | collective-permute-start | bytes 10813448 | tf_op jit(solution)/shard_map/ppermute | solution.py:16
  515.4 177.1 %collective-permute-start.1 = (bf16[2,2,1408,352]{2,3,1,0:T(8,128)(2,1)}, bf16[2,2,1408,352]{2,3,1,0:T(8,128)(2,1)}, u32[]{:S(2)}, u32[]{:S(2)}) collective-permute-start(bf16[2,2,1408,352]{2,3,1,0:T(8,128)(2,1)} %all_to_all.50), channel_id=1, source_target_pairs={{0,128},{128,0},{4,132},{132,4},{8,136},{136,8},{12,140},{140,12},... | collective-permute-start | bytes 11894792 | tf_op jit(solution)/shard_map/ppermute | solution.py:16
Sparse Core Ops, SparseCore 0:
  226.2 192.0 all-gather.1
where the time goes:
time: 708 us; the launch traced here: 707 us
  blocking collectives  312 us (44%)
  waiting for transfers between devices  298 us (42%)
  local copies, waits for them, and re-layouts  53.5 us (8%)
  matrix products  17.1 us (2%)
  between operations  13.4 us (2%)
    ppermute x2, waiting for transfers between devices, swapped(): return lax.ppermute(block, axis, route)  269 us
    all_to_all x1, blocking collectives, local(): lax.all_to_all(chol, 'occ', split_axis=1, concat_axis=0, tiled=True)  155 us
    all_to_all x1, blocking collectives, local(): lax.all_to_all(dressed, 'occ', split_axis=1, concat_axis=0, tiled=True)  103 us
    all_to_all x1, blocking collectives, local(): lax.all_to_all(direct, 'vir', split_axis=3, concat_axis=2, tiled=True)  54.3 us
    all_gather x1, waiting for transfers between devices, local(): lax.all_gather(far_x, 'vir', axis=2, tiled=True)  28.5 us
    dot_general x1, matrix products, contract(): jnp.einsum('pia,pjb->ijab', left, right, preferred_element_type=jnp.float32)  17.1 us
  transfers between devices with their start and end apart: 3, of which 3 were waited for; matrix products, arithmetic and copies ran while one was open for 2% of the time, Pallas kernels for 0%

commit v1 on v0

v1 whole, which is shorter than its diff:
```python
import functools

import jax
import jax.numpy as jnp
from jax import lax
from jax.experimental import pallas as pl
from jax.experimental.pallas import tpu as pltpu
from jax.sharding import PartitionSpec as P

SLAB = 16
NZ, NY, NC = 8, 4, 2
PLACES = NZ * NY * NC
STEPS = 8
FIRST = 32
ROWS, GROUPS = 16, 4
PARAMS = pltpu.CompilerParams(vmem_limit_bytes=48 * 1024 * 1024)


def place(z, y, c):
    return ((z % NZ) * NY + y) * NC + c


def centres():
    return [place(low + 2 + 4 * c, y, r) for low in range(4) for y in range(NY) for c in range(NC) for r in range(2)]


def core_route():
    return [(place(z, y, c), place(z, y, 1 - c)) for z in range(NZ) for y in range(NY) for c in range(NC)]


def x_route(bits):
    return [(g, g ^ bits) for g in range(4)]


def home_route(first, k_bits, m_bits):
    route = []
    for low in range(4):
        for c in range(NC):
            for y in range(NY):
                for r in range(NC):
                    to_k = (r == 0) == first
                    here, there = place(low + 2 + 4 * c, y, r), place(low if to_k else low + 4, y, c)
                    bits = k_bits if to_k else m_bits
                    route += [(here * 4 + g, there * 4 + (g ^ bits)) for g in range(4)]
    return route


def pack_body(l_ref, x_ref, one_ref, two_ref):
    quarter = l_ref.shape[-1]
    for side in range(2):
        pair = (l_ref, x_ref) if side == 0 else (x_ref, l_ref)
        rows = [ref[side] for ref in pair]
        for at in range(GROUPS):
            from_row = at % 2 * ROWS
            one_ref[:, side, :, at * quarter : (at + 1) * quarter] = rows[at // 2][:, from_row : from_row + ROWS]
        two_ref[:, side] = jnp.concatenate([row[:, FIRST:] for row in rows], axis=1)


def pack(chol, dressed):
    _, width, rows, quarter = chol.shape
    share = width // STEPS
    sizes = [(ROWS, GROUPS * quarter), (2 * (rows - FIRST), quarter)]
    return pl.pallas_call(
        pack_body,
        grid=(STEPS,),
        in_specs=[pl.BlockSpec((2, share, rows, quarter), lambda n: (0, n, 0, 0))] * 2,
        out_specs=[pl.BlockSpec((share, 2, *size), lambda n: (n, 0, 0, 0)) for size in sizes],
        out_shape=[jax.ShapeDtypeStruct((width, 2, *size), jnp.bfloat16) for size in sizes],
        compiler_params=PARAMS,
        name="pack",
    )(chol, dressed)


def split_body(part_ref, after_ref, k_ref, m_ref):
    k_ref[...], m_ref[...] = part_ref[:, 0], part_ref[:, 1]


def split(part, after):
    width, _, rows, lanes = part.shape
    share = width // 4
    half = pl.BlockSpec((share, rows, lanes), lambda n: (n, 0, 0))
    return pl.pallas_call(
        split_body,
        grid=(4,),
        in_specs=[pl.BlockSpec((share, 2, rows, lanes), lambda n: (n, 0, 0, 0)), pl.BlockSpec(memory_space=pl.ANY)],
        out_specs=[half] * 2,
        out_shape=[jax.ShapeDtypeStruct((width, rows, lanes), jnp.bfloat16)] * 2,
        compiler_params=PARAMS,
        name="split",
    )(part, after)


def in_lanes(ref, tiles):
    quarter = tiles[0].shape[1]
    at = 0
    for tile in tiles:
        for half in range(2):
            ref[:, at : at + quarter] = tile[half * quarter // 2 : (half + 1) * quarter // 2]
            at += quarter


def finish_near(core, total, first_ref, second_ref):
    straight = [total[e].astype(jnp.bfloat16) for e in range(2)]
    turned = [total[e].T.astype(jnp.bfloat16) for e in range(2)]

    @pl.when(core == 0)
    def _():
        in_lanes(first_ref, straight)
        in_lanes(second_ref, turned)

    @pl.when(core == 1)
    def _():
        in_lanes(first_ref, turned[::-1])
        in_lanes(second_ref, straight[::-1])


def finish_far(core, total, first_ref, second_ref, first_far, second_far):
    tiles = [[total[3 * e + at].astype(jnp.bfloat16) for e in range(2)] for at in range(3)]
    turned = [[total[3 * e + at].T.astype(jnp.bfloat16) for e in range(2)] for at in range(3)]
    (op, po, pp), (op_t, po_t, pp_t) = tiles, turned

    @pl.when(core == 0)
    def _():
        in_lanes(first_ref, op)
        in_lanes(second_ref, po_t)
        for e in range(2):
            in_lanes(first_far.at[e], (po[e], pp[e]))
            in_lanes(second_far.at[e], (op_t[e], pp_t[e]))

    @pl.when(core == 1)
    def _():
        in_lanes(second_ref, op[::-1])
        in_lanes(first_ref, po_t[::-1])
        for e in range(2):
            in_lanes(second_far.at[1 - e], (po[e], pp[e]))
            in_lanes(first_far.at[1 - e], (op_t[e], pp_t[e]))


def tiles_body(n_ops, combos, carried, finish, core_ref, *refs):
    ops, refs = refs[:n_ops], refs[n_ops:]
    if carried:
        before, refs = refs[0], refs[1:]
    total = refs[-1] if finish else refs[0]
    step = pl.program_id(0)

    @pl.when(step == 0)
    def _():
        total[...] = before[...] if carried else jnp.zeros_like(total)

    quarter = total.shape[-1]
    blocks = []
    for op in ops:
        lanes = [op[:, :, at : at + quarter].reshape(-1, quarter) for at in range(0, op.shape[-1], quarter)]
        blocks.append(lanes[0] if len(lanes) == 1 else jnp.concatenate(lanes, axis=0))
    for at, (left, right) in enumerate(combos):
        total[at] += lax.dot_general(
            blocks[left], blocks[right], (((0,), (0,)), ((), ())), preferred_element_type=jnp.float32
        )
    if finish:

        @pl.when(step == pl.num_programs(0) - 1)
        def _():
            finish(core_ref[0], total, *refs[:-1])


def tiles(name, quarter, core, ops, combos, before=None, finish=None):
    specs, arrays = [], []
    for op in ops:
        array, side = op if isinstance(op, tuple) else (op, None)
        width, rows, lanes = array.shape[0], array.shape[-2], array.shape[-1]
        share = 512 * quarter // (rows * lanes)
        if side is None:
            specs.append(pl.BlockSpec((share, rows, lanes), lambda n: (n, 0, 0)))
        else:
            specs.append(pl.BlockSpec((share, None, rows, lanes), lambda n, s=side: (n, s, 0, 0)))
        arrays.append(array)
    sums = (len(combos), quarter, quarter)
    if before is not None:
        specs.append(pl.BlockSpec(sums, lambda n: (0, 0, 0)))
        arrays.append(before)
    if finish is None:
        shapes, scratch = [sums], []
        kind = jnp.float32
    else:
        near = (quarter // 2, 4 * quarter)
        shapes = [near] * 2 if finish is finish_near else [near] * 2 + [(2,) + near] * 2
        scratch = [pltpu.VMEM(sums, jnp.float32)]
        kind = jnp.bfloat16
    return pl.pallas_call(
        functools.partial(tiles_body, len(ops), combos, before is not None, finish),
        grid=(width // share,),
        in_specs=[pl.BlockSpec(memory_space=pltpu.SMEM)] + specs,
        out_specs=[pl.BlockSpec(shape, lambda n, k=len(shape): (0,) * k) for shape in shapes],
        out_shape=[jax.ShapeDtypeStruct(shape, kind) for shape in shapes],
        scratch_shapes=scratch,
        compiler_params=PARAMS,
        name=name,
    )(core, *arrays)


def home_body(where_ref, pairs_ref, mask_ref, *refs):
    sets, out_ref = (refs[:3], refs[3:6]), refs[6]
    is_k, g = where_ref[0], where_ref[1]
    u, v = pl.program_id(0), pl.program_id(1)
    use = jnp.where(is_k == 1, v, 1 - u)
    i = jnp.where(is_k == 1, u, v)
    quarter = out_ref.shape[2]
    scale = pairs_ref[u, v].astype(jnp.float32).astype(jnp.bfloat16)
    half = quarter // 2
    for q in range(4):
        for at in range(2):
            near, side, far = sets[at]
            bits = q ^ g
            from_side = bits == jnp.where(is_k == 1, 3, 1)
            from_far = bits == jnp.where(is_k == 1, 1, 3)
            for this, ref, lane in (
                ((bits == 0) & (i == 0), near, 0),
                ((bits == 0) & (i == 1), near, 2),
                (from_side & (i == 0), side, 0),
                (from_side & (i == 1), side, 2),
                (from_far, far.at[i], 0),
                (bits == 2, far.at[i], 2),
            ):

                @pl.when((use == at) & this)
                def _():
                    for top in range(2):
                        rows = slice(top * half, (top + 1) * half)
                        lanes = slice(q * quarter, (q + 1) * quarter)
                        tile = ref[:, (lane + top) * quarter : (lane + top + 1) * quarter]
                        out_ref[0, 0, rows, lanes] = tile * (mask_ref[rows, lanes] * scale)


def home(where, pairs, mask, arrays):
    quarter, whole = mask.shape
    full = [pl.BlockSpec(a.shape, lambda u, v, k=a.ndim: (0,) * k) for a in (mask, *arrays)]
    return pl.pallas_call(
        home_body,
        grid=(2, 2),
        in_specs=[pl.BlockSpec(memory_space=pltpu.SMEM)] * 2 + full,
        out_specs=pl.BlockSpec((1, 1, quarter, whole), lambda u, v: (u, v, 0, 0)),
        out_shape=jax.ShapeDtypeStruct((2, 2, quarter, whole), jnp.bfloat16),
        compiler_params=PARAMS,
        name="home",
    )(where, pairs, mask, *arrays)


def local(chol, dressed, pair_mask, sym_mask):
    rows, orbitals, quarter = chol.shape
    occ, g = lax.axis_index("occ"), lax.axis_index("vir")
    core = (occ % NC).astype(jnp.int32).reshape(1)
    order = [centres()]

    turned = [jnp.transpose(a, (1, 0, 2)).reshape(2, PLACES, rows, quarter) for a in (chol, dressed)]
    packed = pack(*turned)
    got = [lax.all_to_all(part, "occ", 0, 0, axis_index_groups=order, tiled=True) for part in packed]

    def spread(k, m):
        k_core = lax.ppermute(k, "occ", core_route())
        k_x = lax.ppermute(k, "vir", x_route(1))
        m_x = lax.ppermute(m, "vir", x_route(3))
        return k_core, k_x, lax.ppermute(k_x, "occ", core_route()), m_x

    near_combos = ((0, 2), (1, 2))
    rest_combos = ((0, 5), (2, 4), (2, 5), (1, 5), (3, 4), (3, 5))

    def near_ops(part, k_core):
        return [(part, 0), k_core, (part, 1)]

    def rest_ops(part, k_core, k_x, k_both, m_x):
        return [(part, 0), k_core, k_x, k_both, (part, 1), m_x]

    one = spread(got[0][:, 0], got[0][:, 1])
    (near,) = tiles("near", quarter, core, near_ops(got[0], one[0]), near_combos)
    two = spread(*split(got[1], near))
    near = tiles("near", quarter, core, near_ops(got[1], two[0]), near_combos, near, finish_near)
    (rest,) = tiles("rest", quarter, core, rest_ops(got[0], *one), rest_combos)
    rest = tiles("rest", quarter, core, rest_ops(got[1], *two), rest_combos, rest, finish_far)

    sent = []
    for is_first in (True, False):
        at = 0 if is_first else 1
        straight, across = home_route(is_first, 0, 0), home_route(is_first, 1, 3)
        axes = ("occ", "vir")
        sent += [
            lax.ppermute(near[at], axes, straight),
            lax.ppermute(rest[at], axes, straight),
            lax.ppermute(rest[2 + at], axes, across),
        ]

    mirror = (occ + PLACES // 2) % PLACES
    pairs = lax.dynamic_slice(pair_mask, (occ * 2, mirror * 2), (2, 2))
    rows_per = quarter // SLAB
    sym_rows = lax.dynamic_slice_in_dim(sym_mask, g * rows_per, rows_per, 0)
    mask = jnp.repeat(jnp.repeat(sym_rows.astype(jnp.bfloat16), SLAB, 0), SLAB, 1)
    where = jnp.stack([(occ < PLACES // 2).astype(jnp.int32), g.astype(jnp.int32)])
    return home(where, pairs, mask, sent)


def solution(mesh):
    placed = (P("occ", None, "vir"), P("occ", None, "vir"), P(), P())
    return jax.shard_map(
        local, mesh=mesh, in_specs=placed, out_specs=P("occ", None, "vir", None), check_vma=False
    )
```

time: 708 us -> 387 us (0.55)
  blocking collectives: 312 us -> 142 us
  waiting for transfers between devices: 298 us -> 134 us
  Pallas kernels: 0 us -> 57 us
  local copies, waits for them, and re-layouts: 53.5 us -> 22.5 us
  starting transfers between devices: 6.09 us -> 27.1 us
  matrix products: 17.1 us -> 0 us
  between operations: 13.4 us -> 0.09 us
    all_to_all x3 -> x1, blocking collectives: 312 us -> 142 us  [local(): lax.all_to_all(part, 'occ', 0, 0, axis_index_groups=order, tiled=True)]
    ppermute x2 -> x14, waiting for transfers between devices: 269 us -> 134 us  [the longest x2 67.8 us: spread(): k_x = lax.ppermute(k, 'vir', x_route(1))]
    pallas_call x0 -> x7, Pallas kernels: none -> 57 us  [the longest x4 41.8 us: tiles(): pl.pallas_call(functools.partial(tiles_body, len(ops), combos, before is...]
    all_gather x1 -> x0, waiting for transfers between devices: 28.5 us -> none  [local(): lax.all_gather(far_x, 'vir', axis=2, tiled=True)]
    all_to_all x5 -> x0, local copies, waits for them, and re-layouts: 24.1 us -> none  [the longest x2 13.4 us: local(): lax.all_to_all(direct, 'vir', split_axis=3, concat_axis=2, tiled=True)]
    dot_general x1 -> x0, matrix products: 17.1 us -> none  [contract(): jnp.einsum('pia,pjb->ijab', left, right, preferred_element_type=jnp.float32)]
    convert_element_type x3 -> x0, local copies, waits for them, and re-layouts: 14.7 us -> none  [the longest x1 12.4 us: local(): contract(own_l, lax.all_gather(far_x, 'vir', axis=2, tiled=True))]
    ppermute x2 -> x14, starting transfers between devices: 6.09 us -> 20 us  [the longest x2 5.68 us: local(): lax.ppermute(rest[2 + at], axes, across)]
  transfers between devices with their start and end apart: 3 -> 15, of which waited for: 3 -> 5; matrix products, arithmetic and copies ran while one was open for 2% -> 1% of each run, Pallas kernels for 0% -> 11%
where the time goes in v1:
time: 387 us; the launch traced here: 383 us
  blocking collectives  142 us (37%)
  waiting for transfers between devices  134 us (35%)
  Pallas kernels  57 us (15%)
  starting transfers between devices  27.1 us (7%)
  local copies, waits for them, and re-layouts  22.5 us (6%)
    all_to_all x1, blocking collectives, local(): lax.all_to_all(part, 'occ', 0, 0, axis_index_groups=order, tiled=True)  142 us
    ppermute x2, waiting for transfers between devices, spread(): k_x = lax.ppermute(k, 'vir', x_route(1))  67.8 us
    ppermute x2, waiting for transfers between devices, local(): lax.ppermute(near[at], axes, straight)  60.6 us
    pallas_call x4, Pallas kernels, tiles(): pl.pallas_call(functools.partial(tiles_body, len(ops), combos, before is...  41.8 us
    transpose x2, local copies, waits for them, and re-layouts, local(): jnp.transpose(a, (1, 0, 2)).reshape(2, PLACES, rows, quarter)  12.5 us
    pallas_call x1, Pallas kernels, pack(): pl.pallas_call(pack_body, grid=(STEPS,), in_specs=[pl.BlockSpec((2, share...  7.92 us
  transfers between devices with their start and end apart: 15, of which 5 were waited for; matrix products, arithmetic and copies ran while one was open for 1% of the time, Pallas kernels for 11%

profile of v1, /device:TPU:8, one launch (start us, length us, event | category | flops | bytes accessed | tf_op | source)
XLA Modules:
  0.0 383.1 jit_solution(15882306665149223604)
XLA Ops:
  0.0 6.2 %copy.31 = bf16[128,40,352]{2,1,0:T(8,128)(2,1)} copy(bf16[128,40,352]{0,2,1:T(8,128)(2,1)} %bitcast.20) | data formatting | bytes 7208960 | tf_op jit(solution)/shard_map/transpose | solution.py:254
  6.2 6.3 %copy.32 = bf16[128,40,352]{2,1,0:T(8,128)(2,1)} copy(bf16[128,40,352]{0,2,1:T(8,128)(2,1)} %bitcast.21) | data formatting | bytes 7208960 | tf_op jit(solution)/shard_map/transpose | solution.py:254
  12.5 0.0 copy-start.1
  12.5 2.1 copy-done.1
  14.6 7.9 %pack.1 = (bf16[64,2,16,1408]{3,2,1,0:T(8,128)(2,1)}, bf16[64,2,16,352]{3,2,1,0:T(8,128)(2,1)}) custom-call(bf16[2,64,40,352]{3,2,1,0:T(8,128)(2,1)S(1)} %bitcast.17, bf16[2,64,40,352]{3,2,1,0:T(8,128)(2,1)} %bitcast.18), custom_call_target="tpu_custom_call" | custom-call | tf_op jit(solution)/shard_map/pack/pallas_call | solution.py:63
  22.6 141.8 %all_to_all.10.refs_0_.refs_2_.refs_4_ = bf16[64,2,16,1408]{3,2,1,0:T(8,128)(2,1)S(1)} all-to-all(bf16[64,2,16,1408]{3,2,1,0:T(8,128)(2,1)} %get-tuple-element.16), channel_id=1, replica_groups={{64,68,192,196,72,76,200,204,80,84,208,212,88,92,216,220,96,100,224,228..., dimensions={0} | all-to-all | bytes 11534336 | tf_op jit(solution)/shard_map/all_to_all | solution.py:256
  164.4 0.0 copy-start.2
  164.4 3.2 slice_bitcast_fusion
  167.5 1.0 copy-done.2
  168.6 1.5 collective-permute-start.6
  170.1 0.0 collective-permute-start
  170.1 7.1 %all-to-all-start = ((bf16[64,2,16,352]{3,2,1,0:T(8,128)(2,1)}), bf16[64,2,16,352]{3,2,1,0:T(8,128)(2,1)S(1)}, u32[]{:S(2)}, u32[]{:S(2)}) async-start(bf16[64,2,16,352]{3,2,1,0:T(8,128)(2,1)} %get-tuple-element.15), calls=%async_computation | async-start | bytes 3145728 | tf_op jit(solution)/shard_map/all_to_all | solution.py:256
  177.2 2.2 collective-permute-start.8
  179.4 51.6 %collective-permute-done.6.refs_2_ = bf16[64,16,1408]{2,1,0:T(8,128)(2,1)} collective-permute-done((bf16[64,16,1408]{2,1,0:T(8,128)(2,1)}, bf16[64,16,1408]{2,1,0:T(8,128)(2,1)}, u32[]{:S(2)}, u32[]{:S(2)}) %collective-permute-start.6) | collective-permute-done | bytes 2883616 | tf_op jit(solution)/shard_map/ppermute | solution.py:260
  231.0 0.0 collective-permute-start.7
  231.0 0.0 collective-permute-done.refs_1_
  231.0 10.4 %near.2.after_ref.refs_3_ = f32[2,352,352]{2,1,0:T(8,128)S(1)} custom-call(s32[1]{0:T(128)} %bitcast.4.core_ref, bf16[64,2,16,1408]{3,2,1,0:T(8,128)(2,1)} %copy-done.2, bf16[64,16,1408]{2,1,0:T(8,128)(2,1)} %collective-permute-done.refs_1_, bf16[64,2,16,1408]{3,2,1,0:T(8,128)(2,1)} %copy-done.2), custom_call_target="tpu_custom_call" | custom-call | tf_op jit(solution)/shard_map/near/pallas_call | solution.py:189
  241.4 0.0 all-to-all-done.part_ref.refs_0_.refs_2_.refs_4_
  241.5 0.0 copy-start
  241.5 0.2 split.1
  241.7 1.6 collective-permute-start.3
  243.3 0.2 collective-permute-start.1
  243.5 2.1 collective-permute-start.5
  245.6 16.1 %collective-permute-done.3.refs_2_ = bf16[64,16,352]{2,1,0:T(8,128)(2,1)S(1)} collective-permute-done((bf16[64,16,352]{2,1,0:T(8,128)(2,1)S(1)}, bf16[64,16,352]{2,1,0:T(8,128)(2,1)S(1)}, u32[]{:S(2)}, u32[]{:S(2)}) %collective-permute-start.3) | collective-permute-done | bytes 720928 | tf_op jit(solution)/shard_map/ppermute | solution.py:260
  261.7 0.0 collective-permute-start.4
  261.7 0.0 collective-permute-done.1.refs_1_
  261.7 2.8 near.3
  264.5 0.0 copy-done
  264.5 3.3 collective-permute-start.11
  267.8 0.0 collective-permute-done.8.refs_5_
  267.8 0.0 collective-permute-done.7.refs_3_
  267.8 20.4 %rest.2.refs_6_ = f32[6,352,352]{2,1,0:T(8,128)} custom-call(s32[1]{0:T(128)} %bitcast.4.core_ref, bf16[64,2,16,1408]{3,2,1,0:T(8,128)(2,1)} %copy-done.2, bf16[64,16,1408]{2,1,0:T(8,128)(2,1)} %collective-permute-done.refs_1_, bf16[64,16,1408]{2,1,0:T(8,128)(2,1)} %collective-permute-done.6.refs_2_, bf16[64,16,1408]{2,1,0:T(8,128)(2,1)} %collective-permute-done.7.refs_3_, ...), custom_call_target="tpu_custom_call" | custom-call | tf_op jit(solution)/shard_map/rest/pallas_call | solution.py:189
  288.2 0.0 collective-permute-done.5.refs_5_
  288.2 0.0 collective-permute-done.4.refs_3_
  288.2 8.3 %rest.3 = (bf16[176,1408]{1,0:T(8,128)(2,1)}, bf16[176,1408]{1,0:T(8,128)(2,1)}, bf16[2,176,1408]{2,1,0:T(8,128)(2,1)}, bf16[2,176,1408]{2,1,0:T(8,128)(2,1)}) custom-call(s32[1]{0:T(128)} %bitcast.4.core_ref, bf16[64,2,16,352]{3,2,1,0:T(8,128)(2,1)} %copy-done, bf16[64,16,352]{2,1,0:T(8,128)(2,1)S(1)} %collective-permute-done.1.refs_1_, ...), custom_call_target="tpu_custom_call" | custom-call | tf_op jit(solution)/shard_map/rest/pallas_call | solution.py:189
  296.5 1.1 collective-permute-start.10
  297.6 4.6 %collective-permute-start.13 = (bf16[2,176,1408]{2,1,0:T(8,128)(2,1)}, bf16[2,176,1408]{2,1,0:T(8,128)(2,1)S(1)}, u32[]{:S(2)}, u32[]{:S(2)}) collective-permute-start(bf16[2,176,1408]{2,1,0:T(8,128)(2,1)} %get-tuple-element.24), channel_id=1, source_target_pairs={{64,131},{65,130},{66,129},{67,128},{68,1},{69,0},{70,3},{71,2},{7... | collective-permute-start | bytes 2973704 | tf_op jit(solution)/shard_map/ppermute | solution.py:288
  302.2 0.0 collective-permute-start.2
  302.2 1.7 collective-permute-start.12
  303.9 0.0 collective-permute-done.11.refs_3_
  303.9 1.7 collective-permute-start.9
  305.6 0.7 dynamic-slice_convert_fusion
  306.3 0.1 copy.30
  306.5 1.1 broadcast_in_dim.7
  307.5 1.7 copy.35.mask_ref
  309.2 0.8 dynamic_slice.6.pairs_ref
  310.0 0.1 pad_add_fusion.where_ref
  310.1 60.6 %collective-permute-done.2.refs_0_ = bf16[176,1408]{1,0:T(8,128)(2,1)} collective-permute-done((bf16[176,1408]{1,0:T(8,128)(2,1)}, bf16[176,1408]{1,0:T(8,128)(2,1)}, u32[]{:S(2)}, u32[]{:S(2)}) %collective-permute-start.2) | collective-permute-done | bytes 495648 | tf_op jit(solution)/shard_map/ppermute | solution.py:286
  370.7 0.1 collective-permute-done.12.refs_4_
  370.8 5.3 %collective-permute-done.9.refs_1_ = bf16[176,1408]{1,0:T(8,128)(2,1)} collective-permute-done((bf16[176,1408]{1,0:T(8,128)(2,1)}, bf16[176,1408]{1,0:T(8,128)(2,1)}, u32[]{:S(2)}, u32[]{:S(2)}) %collective-permute-start.9) | collective-permute-done | bytes 495648 | tf_op jit(solution)/shard_map/ppermute | solution.py:287
  376.1 0.0 collective-permute-done.10.refs_2_
  376.1 0.0 collective-permute-done.13.refs_5_
  376.1 7.0 %home.1 = bf16[2,2,352,1408]{3,2,1,0:T(8,128)(2,1)} custom-call(s32[2]{0:T(128)S(1)} %pad_add_fusion.where_ref, s32[2,2]{1,0:T(2,128)S(1)} %dynamic_slice.6.pairs_ref, bf16[352,1408]{1,0:T(8,128)(2,1)S(1)} %copy.35.mask_ref, bf16[176,1408]{1,0:T(8,128)(2,1)} %collective-permute-done.2.refs_0_, bf16[176,1408]{1,0:T(8,128)(2,1)} %collective-permute-done.9.refs_1_, ...), custom_call_target="tpu_custom_call" | custom-call | tf_op jit(solution)/shard_map/home/pallas_call | solution.py:237
  (1 shorter events, 0.0 us)
Async XLA Ops:
  12.5 2.1 copy-start.1
  164.4 4.2 %copy-start.2 = (bf16[64,2,16,1408]{3,2,1,0:T(8,128)(2,1)}, bf16[64,2,16,1408]{3,2,1,0:T(8,128)(2,1)S(1)}, u32[]{:S(2)}) copy-start(bf16[64,2,16,1408]{3,2,1,0:T(8,128)(2,1)S(1)} %all_to_all.10.refs_0_.refs_2_.refs_4_) | copy-start | bytes 17301508
  168.6 62.5 %collective-permute-start.6 = (bf16[64,16,1408]{2,1,0:T(8,128)(2,1)}, bf16[64,16,1408]{2,1,0:T(8,128)(2,1)}, u32[]{:S(2)}, u32[]{:S(2)}) collective-permute-start(bf16[64,16,1408]{2,1,0:T(8,128)(2,1)} %get-tuple-element.26), channel_id=1, source_target_pairs={{0,1},{1,0},{2,3},{3,2},{4,5},{5,4},{6,7},{7,6},{8,9},{9,8},{10,11... | collective-permute-start | bytes 8650760 | tf_op jit(solution)/shard_map/ppermute | solution.py:260
  170.1 61.0 %collective-permute-start = (bf16[64,16,1408]{2,1,0:T(8,128)(2,1)}, bf16[64,16,1408]{2,1,0:T(8,128)(2,1)}, u32[]{:S(2)}, u32[]{:S(2)}) collective-permute-start(bf16[64,16,1408]{2,1,0:T(8,128)(2,1)} %get-tuple-element.26), channel_id=1, source_target_pairs={{0,4},{4,0},{8,12},{12,8},{16,20},{20,16},{24,28},{28,24},{32,36},... | collective-permute-start | bytes 8650760 | tf_op jit(solution)/shard_map/ppermute | solution.py:259
  170.1 71.4 %all-to-all-start = ((bf16[64,2,16,352]{3,2,1,0:T(8,128)(2,1)}), bf16[64,2,16,352]{3,2,1,0:T(8,128)(2,1)S(1)}, u32[]{:S(2)}, u32[]{:S(2)}) async-start(bf16[64,2,16,352]{3,2,1,0:T(8,128)(2,1)} %get-tuple-element.15), calls=%async_computation | async-start | bytes 3145728 | tf_op jit(solution)/shard_map/all_to_all | solution.py:256
  177.2 90.6 %collective-permute-start.8 = (bf16[64,16,1408]{2,1,0:T(8,128)(2,1)}, bf16[64,16,1408]{2,1,0:T(8,128)(2,1)}, u32[]{:S(2)}, u32[]{:S(2)}) collective-permute-start(bf16[64,16,1408]{2,1,0:T(8,128)(2,1)} %get-tuple-element.25), channel_id=1, source_target_pairs={{0,3},{1,2},{2,1},{3,0},{4,7},{5,6},{6,5},{7,4},{8,11},{9,10},{10,... | collective-permute-start | bytes 8650760 | tf_op jit(solution)/shard_map/ppermute | solution.py:261
  231.0 36.8 %collective-permute-start.7 = (bf16[64,16,1408]{2,1,0:T(8,128)(2,1)}, bf16[64,16,1408]{2,1,0:T(8,128)(2,1)}, u32[]{:S(2)}, u32[]{:S(2)}) collective-permute-start(bf16[64,16,1408]{2,1,0:T(8,128)(2,1)} %collective-permute-done.6.refs_2_), channel_id=1, source_target_pairs={{0,4},{4,0},{8,12},{12,8},{16,20},{20,16},{24,28},{28,24},{32,36},... | collective-permute-start | bytes 8650760 | tf_op jit(solution)/shard_map/ppermute | solution.py:262
  241.5 23.0 %copy-start = (bf16[64,2,16,352]{3,2,1,0:T(8,128)(2,1)}, bf16[64,2,16,352]{3,2,1,0:T(8,128)(2,1)S(1)}, u32[]{:S(2)}) copy-start(bf16[64,2,16,352]{3,2,1,0:T(8,128)(2,1)S(1)} %all-to-all-done.part_ref.refs_0_.refs_2_.refs_4_) | copy-start | bytes 4325380
  241.7 20.0 %collective-permute-start.3 = (bf16[64,16,352]{2,1,0:T(8,128)(2,1)S(1)}, bf16[64,16,352]{2,1,0:T(8,128)(2,1)S(1)}, u32[]{:S(2)}, u32[]{:S(2)}) collective-permute-start(bf16[64,16,352]{2,1,0:T(8,128)(2,1)S(1)} %get-tuple-element.17), channel_id=1, source_target_pairs={{0,1},{1,0},{2,3},{3,2},{4,5},{5,4},{6,7},{7,6},{8,9},{9,8},{10,11... | collective-permute-start | bytes 2162696 | tf_op jit(solution)/shard_map/ppermute | solution.py:260
  243.3 18.5 %collective-permute-start.1 = (bf16[64,16,352]{2,1,0:T(8,128)(2,1)S(1)}, bf16[64,16,352]{2,1,0:T(8,128)(2,1)S(1)}, u32[]{:S(2)}, u32[]{:S(2)}) collective-permute-start(bf16[64,16,352]{2,1,0:T(8,128)(2,1)S(1)} %get-tuple-element.17), channel_id=1, source_target_pairs={{0,4},{4,0},{8,12},{12,8},{16,20},{20,16},{24,28},{28,24},{32,36},... | collective-permute-start | bytes 2162696 | tf_op jit(solution)/shard_map/ppermute | solution.py:259
  243.5 44.7 %collective-permute-start.5 = (bf16[64,16,352]{2,1,0:T(8,128)(2,1)S(1)}, bf16[64,16,352]{2,1,0:T(8,128)(2,1)S(1)}, u32[]{:S(2)}, u32[]{:S(2)}) collective-permute-start(bf16[64,16,352]{2,1,0:T(8,128)(2,1)S(1)} %get-tuple-element.19), channel_id=1, source_target_pairs={{0,3},{1,2},{2,1},{3,0},{4,7},{5,6},{6,5},{7,4},{8,11},{9,10},{10,... | collective-permute-start | bytes 2162696 | tf_op jit(solution)/shard_map/ppermute | solution.py:261
  261.7 26.5 %collective-permute-start.4 = (bf16[64,16,352]{2,1,0:T(8,128)(2,1)S(1)}, bf16[64,16,352]{2,1,0:T(8,128)(2,1)S(1)}, u32[]{:S(2)}, u32[]{:S(2)}) collective-permute-start(bf16[64,16,352]{2,1,0:T(8,128)(2,1)S(1)} %collective-permute-done.3.refs_2_), channel_id=1, source_target_pairs={{0,4},{4,0},{8,12},{12,8},{16,20},{20,16},{24,28},{28,24},{32,36},... | collective-permute-start | bytes 2162696 | tf_op jit(solution)/shard_map/ppermute | solution.py:262
  264.5 39.4 %collective-permute-start.11 = (bf16[176,1408]{1,0:T(8,128)(2,1)S(1)}, bf16[176,1408]{1,0:T(8,128)(2,1)S(1)}, u32[]{:S(2)}, u32[]{:S(2)}) collective-permute-start(bf16[176,1408]{1,0:T(8,128)(2,1)S(1)} %get-tuple-element.22), channel_id=1, source_target_pairs={{64,128},{65,129},{66,130},{67,131},{68,0},{69,1},{70,2},{71,3},{7... | collective-permute-start | bytes 1486856 | tf_op jit(solution)/shard_map/ppermute | solution.py:286
  296.5 79.6 %collective-permute-start.10 = (bf16[2,176,1408]{2,1,0:T(8,128)(2,1)}, bf16[2,176,1408]{2,1,0:T(8,128)(2,1)S(1)}, u32[]{:S(2)}, u32[]{:S(2)}) collective-permute-start(bf16[2,176,1408]{2,1,0:T(8,128)(2,1)} %get-tuple-element.21), channel_id=1, source_target_pairs={{64,1},{65,0},{66,3},{67,2},{68,131},{69,130},{70,129},{71,128},{7... | collective-permute-start | bytes 2973704 | tf_op jit(solution)/shard_map/ppermute | solution.py:288
  297.6 78.5 %collective-permute-start.13 = (bf16[2,176,1408]{2,1,0:T(8,128)(2,1)}, bf16[2,176,1408]{2,1,0:T(8,128)(2,1)S(1)}, u32[]{:S(2)}, u32[]{:S(2)}) collective-permute-start(bf16[2,176,1408]{2,1,0:T(8,128)(2,1)} %get-tuple-element.24), channel_id=1, source_target_pairs={{64,131},{65,130},{66,129},{67,128},{68,1},{69,0},{70,3},{71,2},{7... | collective-permute-start | bytes 2973704 | tf_op jit(solution)/shard_map/ppermute | solution.py:288
  302.2 68.5 %collective-permute-start.2 = (bf16[176,1408]{1,0:T(8,128)(2,1)}, bf16[176,1408]{1,0:T(8,128)(2,1)}, u32[]{:S(2)}, u32[]{:S(2)}) collective-permute-start(bf16[176,1408]{1,0:T(8,128)(2,1)} %get-tuple-element.18), channel_id=1, source_target_pairs={{64,0},{65,1},{66,2},{67,3},{68,128},{69,129},{70,130},{71,131},{7... | collective-permute-start | bytes 1486856 | tf_op jit(solution)/shard_map/ppermute | solution.py:286
  302.2 68.6 %collective-permute-start.12 = (bf16[176,1408]{1,0:T(8,128)(2,1)}, bf16[176,1408]{1,0:T(8,128)(2,1)}, u32[]{:S(2)}, u32[]{:S(2)}) collective-permute-start(bf16[176,1408]{1,0:T(8,128)(2,1)} %get-tuple-element.23), channel_id=1, source_target_pairs={{64,128},{65,129},{66,130},{67,131},{68,0},{69,1},{70,2},{71,3},{7... | collective-permute-start | bytes 1486856 | tf_op jit(solution)/shard_map/ppermute | solution.py:287
  303.9 72.2 %collective-permute-start.9 = (bf16[176,1408]{1,0:T(8,128)(2,1)}, bf16[176,1408]{1,0:T(8,128)(2,1)}, u32[]{:S(2)}, u32[]{:S(2)}) collective-permute-start(bf16[176,1408]{1,0:T(8,128)(2,1)} %get-tuple-element.20), channel_id=1, source_target_pairs={{64,0},{65,1},{66,2},{67,3},{68,128},{69,129},{70,130},{71,131},{7... | collective-permute-start | bytes 1486856 | tf_op jit(solution)/shard_map/ppermute | solution.py:287

commit v2 on v0

v2 whole, which is shorter than its diff:
```python
import functools

import jax
import jax.numpy as jnp
from jax import lax
from jax.experimental import pallas as pl
from jax.experimental.pallas import tpu as pltpu
from jax.sharding import PartitionSpec as P

SLAB = 16
NZ, NY, NC = 8, 4, 2
PLACES = NZ * NY * NC
SUB = 8
SHARE = 16
PARAMS = pltpu.CompilerParams(vmem_limit_bytes=48 * 1024 * 1024)


def place(z, y, c):
    return ((z % NZ) * NY + y) * NC + c


def centres():
    return [place(low + 2 + 4 * c, y, r) for low in range(4) for y in range(NY) for c in range(NC) for r in range(2)]


def core_route():
    return [(place(z, y, c), place(z, y, 1 - c)) for z in range(NZ) for y in range(NY) for c in range(NC)]


def x_route(bits):
    return [(g, g ^ bits) for g in range(4)]


def home_route(first, k_bits, m_bits):
    route = []
    for low in range(4):
        for c in range(NC):
            for y in range(NY):
                for r in range(NC):
                    to_k = (r == 0) == first
                    here, there = place(low + 2 + 4 * c, y, r), place(low if to_k else low + 4, y, c)
                    bits = k_bits if to_k else m_bits
                    route += [(here * 4 + g, there * 4 + (g ^ bits)) for g in range(4)]
    return route


def ceil_lanes(lanes):
    return -(-lanes // 128) * 128


def pieces(quarter, groups, at):
    whole = quarter // 128 * 128
    rest = quarter - whole
    cut = [(slice(0, whole), slice(at * whole, (at + 1) * whole))] if whole else []
    start = groups * whole + at * rest
    return cut + ([(slice(whole, quarter), slice(start, start + rest))] if rest else [])


def pack_body(m_lanes, l_ref, x_ref, one_ref, two_ref):
    quarter = l_ref.shape[1]
    spots = one_ref.shape[0]
    turned = []
    for ref in (l_ref, x_ref):
        block = jnp.swapaxes(jnp.swapaxes(ref[...].astype(jnp.float32), 1, 2), 0, 1)
        turned.append(block.astype(jnp.bfloat16).reshape(2, spots, 2, SUB, quarter))
    step = pl.program_id(0)
    n_groups = two_ref.shape[-1] // quarter
    starts = (0, m_lanes // 2, m_lanes)
    for at in range(n_groups):

        @pl.when(step == at)
        def _():
            for r in range(2):
                blocks = (turned[1 - r][1, :, r], turned[r][1, :, r], turned[r][0, :, 0], turned[r][0, :, 1])
                spots_of = [(one_ref, start) for start in starts] + [(two_ref, 0)]
                for block, (ref, start) in zip(blocks, spots_of):
                    for of, to in pieces(quarter, n_groups, at):
                        ref[:, r, :, start + to.start : start + to.stop] = block[:, :, of]


def pack(chol, dressed):
    rows, quarter, orbitals = chol.shape
    spots, groups = orbitals // 4, rows // SUB
    k_lanes = ceil_lanes(groups * quarter)
    m_lanes = 2 * k_lanes
    shapes = [(spots, 2, SUB, m_lanes + k_lanes), (spots, 2, SUB, k_lanes)]
    one, two = pl.pallas_call(
        functools.partial(pack_body, m_lanes),
        grid=(groups,),
        in_specs=[pl.BlockSpec((SUB, quarter, orbitals), lambda n: (n, 0, 0))] * 2,
        out_specs=[pl.BlockSpec(shape, lambda n: (0, 0, 0, 0)) for shape in shapes],
        out_shape=[jax.ShapeDtypeStruct(shape, jnp.bfloat16) for shape in shapes],
        compiler_params=PARAMS,
        name="pack",
    )(chol, dressed)
    return one.reshape(-1, SUB, m_lanes + k_lanes), two.reshape(-1, SUB, k_lanes), k_lanes


def in_lanes(ref, tile):
    high, wide = tile.shape[0] // 4, tile.shape[1]
    for at in range(4):
        ref[:, at * wide : (at + 1) * wide] = tile[at * high : (at + 1) * high].astype(jnp.bfloat16)


def tiles_body(n_left, n_right, messages, quarter, groups, core_ref, *refs):
    lefts, refs = refs[: 2 * n_left], refs[2 * n_left :]
    rights, refs = refs[: 2 * n_right], refs[2 * n_right :]
    firsts, seconds, total = refs[: len(messages)], refs[len(messages) : -1], refs[-1]
    combos = [combo for message in messages for combo in message]
    spots = [(at, n) for at, message in enumerate(messages) for n in range(len(message))]
    step = pl.program_id(0)

    @pl.when(step == 0)
    def _():
        total[...] = jnp.zeros_like(total)

    def rows(ref):
        blocks = []
        for at in range(groups):
            cut = [ref[:, :, to] for _, to in pieces(quarter, groups, at)]
            cut = [part.reshape(-1, part.shape[-1]) for part in cut]
            blocks.append(jnp.concatenate(cut, axis=1) if len(cut) > 1 else cut[0])
        return jnp.concatenate(blocks, axis=0)

    left, right = [
        [jnp.concatenate([rows(own), rows(far)], axis=0) for own, far in zip(side[::2], side[1::2])]
        for side in (lefts, rights)
    ]
    for at, (i, j) in enumerate(combos):
        total[at] += lax.dot_general(left[i], right[j], (((0,), (0,)), ((), ())), preferred_element_type=jnp.float32)

    @pl.when(step == pl.num_programs(0) - 1)
    def _():
        for at, (message, n) in enumerate(spots):
            straight, turned = total[at], total[at].T
            first, second = firsts[message].at[n], seconds[message].at[n]

            @pl.when(core_ref[0] == 0)
            def _():
                in_lanes(first, straight)
                in_lanes(second, turned)

            @pl.when(core_ref[0] == 1)
            def _():
                in_lanes(first, turned)
                in_lanes(second, straight)


def tiles(name, quarter, core, lefts, rights, messages):
    arrays = [a for pair in (*lefts, *rights) for a in pair]
    width = arrays[0].shape[0]
    groups = arrays[0].shape[-1] // quarter
    shapes = [(len(message), quarter // 4, 4 * quarter) for message in messages] * 2
    out = pl.pallas_call(
        functools.partial(tiles_body, len(lefts), len(rights), messages, quarter, groups),
        grid=(width // SHARE,),
        in_specs=[pl.BlockSpec(memory_space=pltpu.SMEM)]
        + [pl.BlockSpec((SHARE, *a.shape[1:]), lambda n: (n, 0, 0)) for a in arrays],
        out_specs=[pl.BlockSpec(shape, lambda n: (0, 0, 0)) for shape in shapes],
        out_shape=[jax.ShapeDtypeStruct(shape, jnp.bfloat16) for shape in shapes],
        scratch_shapes=[pltpu.VMEM((sum(map(len, messages)), quarter, quarter), jnp.float32)],
        compiler_params=PARAMS,
        name=name,
    )(core, *arrays)
    return list(zip(out[: len(messages)], out[len(messages) :]))


def send(pair, k_bits, m_bits):
    return [
        lax.ppermute(pair[at], ("occ", "vir"), home_route(at == 0, k_bits, m_bits)) for at in range(2)
    ]


def home_body(spots, where_ref, pairs_ref, mask_ref, *refs):
    arrived, out_ref, held = refs[:-2], refs[-2], refs[-1]
    is_k, g = where_ref[0], where_ref[1]
    u, v = pl.program_id(0), pl.program_id(1)
    use = jnp.where(is_k == 1, v, 1 - u)
    i = jnp.where(is_k == 1, u, v)
    quarter = out_ref.shape[2]
    scale = pairs_ref[u, v].astype(jnp.float32).astype(jnp.bfloat16)
    for at in range(2):
        for orbital in range(2):

            @pl.when((use == at) & (i == orbital))
            def _():
                for bits in range(4):
                    ref, index = spots[bits, orbital]
                    ref = arrived[2 * ref + at]
                    parts = [ref[index, :, n * quarter : (n + 1) * quarter].astype(jnp.float32) for n in range(4)]
                    held[bits] = jnp.concatenate(parts, axis=0).astype(jnp.bfloat16)

    for q in range(4):
        lanes = slice(q * quarter, (q + 1) * quarter)
        out_ref[0, 0, :, lanes] = held[q ^ g] * (mask_ref[:, lanes] * scale)


def home(spots, where, pairs, mask, arrays):
    quarter, whole = mask.shape
    full = [pl.BlockSpec(a.shape, lambda u, v, k=a.ndim: (0,) * k) for a in (mask, *arrays)]
    return pl.pallas_call(
        functools.partial(home_body, spots),
        grid=(2, 2),
        in_specs=[pl.BlockSpec(memory_space=pltpu.SMEM)] * 2 + full,
        out_specs=pl.BlockSpec((1, 1, quarter, whole), lambda u, v: (u, v, 0, 0)),
        out_shape=jax.ShapeDtypeStruct((2, 2, quarter, whole), jnp.bfloat16),
        scratch_shapes=[pltpu.VMEM((4, quarter, quarter), jnp.bfloat16)],
        compiler_params=PARAMS,
        name="home",
    )(where, pairs, mask, *arrays)


def local(chol, dressed, pair_mask, sym_mask):
    quarter = chol.shape[2]
    occ, g = lax.axis_index("occ"), lax.axis_index("vir")
    core = (occ % NC).astype(jnp.int32).reshape(1)
    order = [centres()]

    def to_core(part):
        return lax.ppermute(part, "occ", core_route())

    def across(part, bits):
        return lax.ppermute(part, "vir", x_route(bits))

    def after(value, *others):
        return lax.optimization_barrier((value, *others))[0]

    one, two, lanes = pack(*[jnp.transpose(a, (0, 2, 1)) for a in (chol, dressed)])
    one = lax.all_to_all(one, "occ", 0, 0, axis_index_groups=order, tiled=True)
    m_own = one[:, :, :lanes]
    one, two, m_own = lax.optimization_barrier((one, two, m_own))
    m_far, k0 = one[:, :, lanes : 2 * lanes], one[:, :, 2 * lanes :]
    k1 = lax.all_to_all(two, "occ", 0, 0, axis_index_groups=order, tiled=True)

    m_own_x = across(m_own, 3)
    near0, far0 = (k0, to_core(k0)), across(k0, 1)
    m = (m_own, m_far)
    (oo0,) = tiles("first", quarter, core, [near0], [m], [[(0, 0)]])
    got_oo0 = send(oo0, 0, 0)

    far0, k1, m_far = lax.optimization_barrier((far0, k1, m_far, m_own_x, *got_oo0))[:3]
    m_x = (m_own_x, across(m_far, 3))
    near1, far1 = (k1, to_core(k1)), across(k1, 1)
    far0 = (far0, to_core(far0))
    (po0,) = tiles("early", quarter, core, [far0], [m], [[(0, 0)]])
    got_po0 = send(po0, 1, 0)
    (oo1,) = tiles("near", quarter, core, [near1], [m], [[(0, 0)]])
    got_oo1 = send(oo1, 0, 0)

    far1 = after(far1, *got_po0, *got_oo1)
    far1 = (far1, to_core(far1))
    m_x = (m_x[0], after(m_x[1], *got_po0, *got_oo1))
    (op,) = tiles("middle", quarter, core, [near0, near1], [m_x], [[(0, 0), (1, 0)]])
    got_op = send(op, 0, 3)
    far1 = (after(far1[0], *op), far1[1])
    pp0, po1, pp1 = tiles("late", quarter, core, [far0, far1], [m, m_x], [[(0, 1)], [(1, 0)], [(1, 1)]])
    got_pp0, got_po1, got_pp1 = send(pp0, 1, 3), send(po1, 1, 0), send(pp1, 1, 3)
    arrived = [*got_oo0, *got_oo1, *got_po0, *got_po1, *got_pp0, *got_pp1, *got_op]
    spots = {(bits, i): (2 * bits + i, 0) for bits in range(3) for i in range(2)}
    spots |= {(3, i): (6, i) for i in range(2)}

    mirror = (occ + PLACES // 2) % PLACES
    pairs = lax.dynamic_slice(pair_mask, (occ * 2, mirror * 2), (2, 2))
    rows_per = quarter // SLAB
    sym_rows = lax.dynamic_slice_in_dim(sym_mask, g * rows_per, rows_per, 0)
    mask = jnp.repeat(jnp.repeat(sym_rows.astype(jnp.bfloat16), SLAB, 0), SLAB, 1)
    where = jnp.stack([(occ < PLACES // 2).astype(jnp.int32), g.astype(jnp.int32)])
    return home(spots, where, pairs, mask, arrived)


def solution(mesh):
    placed = (P("occ", None, "vir"), P("occ", None, "vir"), P(), P())
    return jax.shard_map(
        local, mesh=mesh, in_specs=placed, out_specs=P("occ", None, "vir", None), check_vma=False
    )
```

time: 708 us -> 354 us (0.50)
  waiting for transfers between devices: 298 us -> 98.4 us
  blocking collectives: 312 us -> 136 us
  Pallas kernels: 0 us -> 54.2 us
  starting transfers between devices: 6.09 us -> 44 us
  local copies, waits for them, and re-layouts: 53.5 us -> 16.5 us
  matrix products: 17.1 us -> 0 us
  between operations: 13.4 us -> 0.15 us
    all_to_all x3 -> x1, blocking collectives: 312 us -> 136 us  [local(): one = lax.all_to_all(one, 'occ', 0, 0, axis_index_groups=order, tiled=True)]
    ppermute x2 -> x22, waiting for transfers between devices: 269 us -> 98.4 us  [the longest x4 64 us: across(): return lax.ppermute(part, 'vir', x_route(bits))]
    pallas_call x0 -> x7, Pallas kernels: none -> 54.2 us  [the longest x5 37.5 us: tiles(): pl.pallas_call(functools.partial(tiles_body, len(lefts), len(rights), mes...]
    ppermute x2 -> x22, starting transfers between devices: 6.09 us -> 36.6 us  [the longest x14 29.4 us: send(): lax.ppermute(pair[at], ('occ', 'vir'), home_route(at == 0, k_bits, m_bits))]
    all_gather x1 -> x0, waiting for transfers between devices: 28.5 us -> none  [local(): lax.all_gather(far_x, 'vir', axis=2, tiled=True)]
    all_to_all x5 -> x0, local copies, waits for them, and re-layouts: 24.1 us -> none  [the longest x2 13.4 us: local(): lax.all_to_all(direct, 'vir', split_axis=3, concat_axis=2, tiled=True)]
    dot_general x1 -> x0, matrix products: 17.1 us -> none  [contract(): jnp.einsum('pia,pjb->ijab', left, right, preferred_element_type=jnp.float32)]
    convert_element_type x3 -> x0, local copies, waits for them, and re-layouts: 14.7 us -> none  [the longest x1 12.4 us: local(): contract(own_l, lax.all_gather(far_x, 'vir', axis=2, tiled=True))]
  transfers between devices with their start and end apart: 3 -> 23, of which waited for: 3 -> 12; matrix products, arithmetic and copies ran while one was open for 2% -> 2% of each run, Pallas kernels for 0% -> 11%
where the time goes in v2:
time: 354 us; the launch traced here: 350 us
  blocking collectives  136 us (38%)
  waiting for transfers between devices  98.4 us (28%)
  Pallas kernels  54.2 us (15%)
  starting transfers between devices  44 us (12%)
  local copies, waits for them, and re-layouts  16.5 us (5%)
    all_to_all x1, blocking collectives, local(): one = lax.all_to_all(one, 'occ', 0, 0, axis_index_groups=order, tiled=True)  136 us
    ppermute x4, waiting for transfers between devices, across(): return lax.ppermute(part, 'vir', x_route(bits))  64 us
    pallas_call x5, Pallas kernels, tiles(): pl.pallas_call(functools.partial(tiles_body, len(lefts), len(rights), mes...  37.5 us
    ppermute x14, waiting for transfers between devices, send(): lax.ppermute(pair[at], ('occ', 'vir'), home_route(at == 0, k_bits, m_bits))  33.4 us
    ppermute x14, starting transfers between devices, send(): lax.ppermute(pair[at], ('occ', 'vir'), home_route(at == 0, k_bits, m_bits))  29.4 us
    pallas_call x1, Pallas kernels, pack(): pl.pallas_call(functools.partial(pack_body, m_lanes), grid=(groups,), in_...  10.3 us
    unnamed x20, local copies, waits for them, and re-layouts  8.52 us
    all_to_all x1, starting transfers between devices, local(): k1 = lax.all_to_all(two, 'occ', 0, 0, axis_index_groups=order, tiled=True)  7.33 us
  transfers between devices with their start and end apart: 23, of which 12 were waited for; matrix products, arithmetic and copies ran while one was open for 2% of the time, Pallas kernels for 11%

profile of v2, /device:TPU:8, one launch (start us, length us, event | category | flops | bytes accessed | tf_op | source)
XLA Modules:
  0.0 350.1 jit_solution(1773606376269884428)
XLA Ops:
  0.0 2.0 copy-done.2
  2.0 10.3 %pack.1 = (bf16[32,2,8,5376]{3,2,1,0:T(8,128)(2,1)}, bf16[32,2,8,1792]{3,2,1,0:T(8,128)(2,1)S(1)}) custom-call(bf16[40,352,128]{2,1,0:T(8,128)(2,1)S(1)} %bitcast.9, bf16[40,352,128]{2,1,0:T(8,128)(2,1)} %bitcast.13), custom_call_target="tpu_custom_call" | custom-call | tf_op jit(solution)/shard_map/pack/pallas_call | solution.py:87
  12.3 136.1 %all_to_all.10 = bf16[64,8,5376]{2,1,0:T(8,128)(2,1)S(1)} all-to-all(bf16[64,8,5376]{2,1,0:T(8,128)(2,1)} %bitcast.11), channel_id=1, replica_groups={{64,68,192,196,72,76,200,204,80,84,208,212,88,92,216,220,96,100,224,228..., dimensions={0} | all-to-all | bytes 11010048 | tf_op jit(solution)/shard_map/all_to_all | solution.py:229
  148.4 0.1 slice.12.refs_2_.refs_4_
  148.5 2.3 copy-done.6
  150.8 7.3 %all-to-all-start.1 = ((bf16[64,8,1792]{2,1,0:T(8,128)(2,1)}), bf16[64,8,1792]{2,1,0:T(8,128)(2,1)}, u32[]{:S(2)}, u32[]{:S(2)}) async-start(bf16[64,8,1792]{2,1,0:T(8,128)(2,1)} %bitcast.10), calls=%async_computation.1 | async-start | bytes 3670016 | tf_op jit(solution)/shard_map/all_to_all | solution.py:233
  158.1 4.2 %fusion = (bf16[64,8,1792]{2,1,0:T(8,128)(2,1)}, bf16[64,8,1792]{2,1,0:T(8,128)(2,1)}) fusion(bf16[64,8,5376]{2,1,0:T(8,128)(2,1)} %copy-done.6), kind=kLoop, calls=%fused_computation.2 | loop fusion | bytes 7340032 | tf_op jit(solution)/shard_map/slice | solution.py:232
  162.4 0.1 collective-permute-start
  162.5 2.8 collective-permute-start.4
  165.3 0.2 collective-permute-start.3
  165.5 1.0 collective-permute-done.refs_1_
  166.5 5.7 %first.1 = (bf16[1,88,1408]{2,1,0:T(8,128)(2,1)S(1)}, bf16[1,88,1408]{2,1,0:T(8,128)(2,1)S(1)}) custom-call(s32[1]{0:T(128)} %bitcast.4.core_ref, bf16[64,8,1792]{2,1,0:T(8,128)(2,1)} %get-tuple-element.56.refs_0_, bf16[64,8,1792]{2,1,0:T(8,128)(2,1)} %collective-permute-done.refs_1_, bf16[64,8,1792]{2,1,0:T(8,128)(2,1)S(1)} %slice.12.refs_2_.refs_4_, ...), custom_call_target="tpu_custom_call" | custom-call | tf_op jit(solution)/shard_map/first/pallas_call | solution.py:154
  172.1 0.3 collective-permute-start.1
  172.4 3.4 collective-permute-start.2
  175.8 30.3 %collective-permute-done.4.refs_4_.refs_6_ = bf16[64,8,1792]{2,1,0:T(8,128)(2,1)} collective-permute-done((bf16[64,8,1792]{2,1,0:T(8,128)(2,1)S(1)}, bf16[64,8,1792]{2,1,0:T(8,128)(2,1)}, u32[]{:S(2)}, u32[]{:S(2)}) %collective-permute-start.4) | collective-permute-done | bytes 1835040 | tf_op jit(solution)/shard_map/ppermute | solution.py:223
  206.1 1.5 collective-permute-done.3.refs_0_
  207.6 1.6 collective-permute-done.1.refs_0_
  209.2 0.0 collective-permute-done.2.refs_1_
  209.2 0.0 all-to-all-done.1.refs_0_.refs_2_
  209.2 0.0 collective-permute-start.8
  209.2 0.5 collective-permute-start.5
  209.7 1.5 collective-permute-start.11
  211.2 2.1 collective-permute-start.12
  213.3 0.0 collective-permute-done.8.refs_1_
  213.3 5.3 %early.1 = (bf16[1,88,1408]{2,1,0:T(8,128)(2,1)S(1)}, bf16[1,88,1408]{2,1,0:T(8,128)(2,1)S(1)}) custom-call(s32[1]{0:T(128)} %bitcast.4.core_ref, bf16[64,8,1792]{2,1,0:T(8,128)(2,1)} %collective-permute-done.3.refs_0_, bf16[64,8,1792]{2,1,0:T(8,128)(2,1)S(1)} %collective-permute-done.8.refs_1_, bf16[64,8,1792]{2,1,0:T(8,128)(2,1)S(1)} %slice.12.refs_2_.refs_4_, ...), custom_call_target="tpu_custom_call" | custom-call | tf_op jit(solution)/shard_map/early/pallas_call | solution.py:154
  218.6 2.9 collective-permute-start.10
  221.5 1.6 collective-permute-start.9
  223.1 0.0 collective-permute-done.5.refs_1_.refs_3_
  223.1 6.0 %near.1 = (bf16[1,88,1408]{2,1,0:T(8,128)(2,1)S(1)}, bf16[1,88,1408]{2,1,0:T(8,128)(2,1)S(1)}) custom-call(s32[1]{0:T(128)} %bitcast.4.core_ref, bf16[64,8,1792]{2,1,0:T(8,128)(2,1)} %all-to-all-done.1.refs_0_.refs_2_, bf16[64,8,1792]{2,1,0:T(8,128)(2,1)S(1)} %collective-permute-done.5.refs_1_.refs_3_, bf16[64,8,1792]{2,1,0:T(8,128)(2,1)S(1)} %slice.12.refs_2_.refs_4_, ...), custom_call_target="tpu_custom_call" | custom-call | tf_op jit(solution)/shard_map/near/pallas_call | solution.py:154
  229.1 1.2 collective-permute-start.6
  230.3 32.2 %collective-permute-done.11.refs_2_ = bf16[64,8,1792]{2,1,0:T(8,128)(2,1)S(1)} collective-permute-done((bf16[64,8,1792]{2,1,0:T(8,128)(2,1)}, bf16[64,8,1792]{2,1,0:T(8,128)(2,1)S(1)}, u32[]{:S(2)}, u32[]{:S(2)}) %collective-permute-start.11) | collective-permute-done | bytes 1835040 | tf_op jit(solution)/shard_map/ppermute | solution.py:223
  262.5 0.0 collective-permute-start.7
  262.5 0.0 collective-permute-done.10.refs_5_
  262.5 0.0 collective-permute-done.9.refs_4_
  262.6 0.0 collective-permute-done.6.refs_2_
  262.6 6.6 %collective-permute-done.7.refs_3_ = bf16[1,88,1408]{2,1,0:T(8,128)(2,1)S(1)} collective-permute-done((bf16[1,88,1408]{2,1,0:T(8,128)(2,1)S(1)}, bf16[1,88,1408]{2,1,0:T(8,128)(2,1)S(1)}, u32[]{:S(2)}, u32[]{:S(2)}) %collective-permute-start.7) | collective-permute-done | bytes 247840 | tf_op jit(solution)/shard_map/ppermute | solution.py:170
  269.2 1.3 copy-done.7
  270.5 8.5 %middle.1 = (bf16[2,88,1408]{2,1,0:T(8,128)(2,1)S(1)}, bf16[2,88,1408]{2,1,0:T(8,128)(2,1)S(1)}) custom-call(s32[1]{0:T(128)} %bitcast.4.core_ref, bf16[64,8,1792]{2,1,0:T(8,128)(2,1)} %get-tuple-element.56.refs_0_, bf16[64,8,1792]{2,1,0:T(8,128)(2,1)} %collective-permute-done.refs_1_, bf16[64,8,1792]{2,1,0:T(8,128)(2,1)} %all-to-all-done.1.refs_0_.refs_2_, ...), custom_call_target="tpu_custom_call" | custom-call | tf_op jit(solution)/shard_map/middle/pallas_call | solution.py:154
  279.0 7.5 %collective-permute-start.20 = (bf16[2,88,1408]{2,1,0:T(8,128)(2,1)S(1)}, bf16[2,88,1408]{2,1,0:T(8,128)(2,1)S(1)}, u32[]{:S(2)}, u32[]{:S(2)}) collective-permute-start(bf16[2,88,1408]{2,1,0:T(8,128)(2,1)S(1)} %get-tuple-element.46), channel_id=1, source_target_pairs={{64,0},{65,1},{66,2},{67,3},{68,131},{69,130},{70,129},{71,128},{7... | collective-permute-start | bytes 1486856 | tf_op jit(solution)/shard_map/ppermute | solution.py:170
  286.5 2.2 collective-permute-start.21
  288.7 1.2 copy-done.9
  290.0 12.0 %late.1 = (bf16[1,88,1408]{2,1,0:T(8,128)(2,1)}, bf16[1,88,1408]{2,1,0:T(8,128)(2,1)S(1)}, bf16[1,88,1408]{2,1,0:T(8,128)(2,1)}, bf16[1,88,1408]{2,1,0:T(8,128)(...) custom-call(s32[1]{0:T(128)} %bitcast.4.core_ref, bf16[64,8,1792]{2,1,0:T(8,128)(2,1)} %collective-permute-done.3.refs_0_, ...), custom_call_target="tpu_custom_call" | custom-call | tf_op jit(solution)/shard_map/late/pallas_call | solution.py:154
  302.0 1.4 collective-permute-start.14
  303.3 0.2 collective-permute-start.15
  303.5 3.3 collective-permute-start.16
  306.9 10.6 %collective-permute-done.20.refs_12_ = bf16[2,88,1408]{2,1,0:T(8,128)(2,1)S(1)} collective-permute-done((bf16[2,88,1408]{2,1,0:T(8,128)(2,1)S(1)}, bf16[2,88,1408]{2,1,0:T(8,128)(2,1)S(1)}, u32[]{:S(2)}, u32[]{:S(2)}) %collective-permute-start.20) | collective-permute-done | bytes 495648 | tf_op jit(solution)/shard_map/ppermute | solution.py:170
  317.5 0.0 collective-permute-start.17
  317.5 0.0 collective-permute-done.21.refs_13_
  317.5 5.5 %collective-permute-start.18 = (bf16[1,88,1408]{2,1,0:T(8,128)(2,1)}, bf16[1,88,1408]{2,1,0:T(8,128)(2,1)}, u32[]{:S(2)}, u32[]{:S(2)}) collective-permute-start(bf16[1,88,1408]{2,1,0:T(8,128)(2,1)} %get-tuple-element.53), channel_id=1, source_target_pairs={{64,1},{65,0},{66,3},{67,2},{68,131},{69,130},{70,129},{71,128},{7... | collective-permute-start | bytes 743432 | tf_op jit(solution)/shard_map/ppermute | solution.py:170
  323.0 0.3 collective-permute-done.14.refs_6_
  323.3 0.7 copy-done.4
  324.0 0.7 dynamic-slice_convert_fusion
  324.8 0.1 copy.7
  324.9 1.1 broadcast_in_dim.7
  326.0 1.7 copy.8.mask_ref
  327.7 0.8 dynamic_slice.6.pairs_ref
  328.4 0.1 pad_add_fusion.where_ref
  328.5 0.0 collective-permute-done.15.refs_7_
  328.5 0.2 collective-permute-done.16.refs_8_
  328.7 9.1 %collective-permute-done.17.refs_9_ = bf16[1,88,1408]{2,1,0:T(8,128)(2,1)} collective-permute-done((bf16[1,88,1408]{2,1,0:T(8,128)(2,1)}, bf16[1,88,1408]{2,1,0:T(8,128)(2,1)}, u32[]{:S(2)}, u32[]{:S(2)}) %collective-permute-start.17) | collective-permute-done | bytes 247840 | tf_op jit(solution)/shard_map/ppermute | solution.py:170
  337.8 1.6 collective-permute-done.18.refs_10_
  339.4 3.3 collective-permute-done.19.refs_11_
  342.8 0.9 copy-done.5
  343.7 6.4 %home.1 = bf16[2,2,352,1408]{3,2,1,0:T(8,128)(2,1)} custom-call(s32[2]{0:T(128)S(1)} %pad_add_fusion.where_ref, s32[2,2]{1,0:T(2,128)S(1)} %dynamic_slice.6.pairs_ref, bf16[352,1408]{1,0:T(8,128)(2,1)S(1)} %copy.8.mask_ref, bf16[1,88,1408]{2,1,0:T(8,128)(2,1)S(1)} %collective-permute-done.1.refs_0_, bf16[1,88,1408]{2,1,0:T(8,128)(2,1)S(1)} %collective-permute-done.2.refs_1_, ...), custom_call_target="tpu_custom_call" | custom-call | tf_op jit(solution)/shard_map/home/pallas_call | solution.py:201
  (19 shorter events, 0.1 us)
Async XLA Ops:
  0.0 2.0 copy-start.2
  12.3 136.1 %copy-start.3 = (bf16[32,2,8,1792]{3,2,1,0:T(8,128)(2,1)}, bf16[32,2,8,1792]{3,2,1,0:T(8,128)(2,1)S(1)}, u32[]{:S(2)}) copy-start(bf16[32,2,8,1792]{3,2,1,0:T(8,128)(2,1)S(1)} %get-tuple-element.31) | copy-start | bytes 5505028
  148.4 2.4 copy-start.6
  150.8 72.3 %copy-start = (bf16[64,8,1792]{2,1,0:T(8,128)(2,1)}, bf16[64,8,1792]{2,1,0:T(8,128)(2,1)S(1)}, u32[]{:S(2)}) copy-start(bf16[64,8,1792]{2,1,0:T(8,128)(2,1)S(1)} %slice.12.refs_2_.refs_4_) | copy-start | bytes 5505028
  150.8 58.4 %all-to-all-start.1 = ((bf16[64,8,1792]{2,1,0:T(8,128)(2,1)}), bf16[64,8,1792]{2,1,0:T(8,128)(2,1)}, u32[]{:S(2)}, u32[]{:S(2)}) async-start(bf16[64,8,1792]{2,1,0:T(8,128)(2,1)} %bitcast.10), calls=%async_computation.1 | async-start | bytes 3670016 | tf_op jit(solution)/shard_map/all_to_all | solution.py:233
  162.4 4.1 %collective-permute-start = (bf16[64,8,1792]{2,1,0:T(8,128)(2,1)}, bf16[64,8,1792]{2,1,0:T(8,128)(2,1)}, u32[]{:S(2)}, u32[]{:S(2)}) collective-permute-start(bf16[64,8,1792]{2,1,0:T(8,128)(2,1)} %get-tuple-element.56.refs_0_), channel_id=1, source_target_pairs={{0,4},{4,0},{8,12},{12,8},{16,20},{20,16},{24,28},{28,24},{32,36},... | collective-permute-start | bytes 5505032 | tf_op jit(solution)/shard_map/ppermute | solution.py:220
  162.5 43.6 %collective-permute-start.4 = (bf16[64,8,1792]{2,1,0:T(8,128)(2,1)S(1)}, bf16[64,8,1792]{2,1,0:T(8,128)(2,1)}, u32[]{:S(2)}, u32[]{:S(2)}) collective-permute-start(bf16[64,8,1792]{2,1,0:T(8,128)(2,1)S(1)} %slice.12.refs_2_.refs_4_), channel_id=1, source_target_pairs={{0,3},{1,2},{2,1},{3,0},{4,7},{5,6},{6,5},{7,4},{8,11},{9,10},{10,... | collective-permute-start | bytes 5505032 | tf_op jit(solution)/shard_map/ppermute | solution.py:223
  165.3 42.3 %collective-permute-start.3 = (bf16[64,8,1792]{2,1,0:T(8,128)(2,1)}, bf16[64,8,1792]{2,1,0:T(8,128)(2,1)}, u32[]{:S(2)}, u32[]{:S(2)}) collective-permute-start(bf16[64,8,1792]{2,1,0:T(8,128)(2,1)} %get-tuple-element.56.refs_0_), channel_id=1, source_target_pairs={{0,1},{1,0},{2,3},{3,2},{4,5},{5,4},{6,7},{7,6},{8,9},{9,8},{10,11... | collective-permute-start | bytes 5505032 | tf_op jit(solution)/shard_map/ppermute | solution.py:223
  172.1 37.0 %collective-permute-start.1 = (bf16[1,88,1408]{2,1,0:T(8,128)(2,1)S(1)}, bf16[1,88,1408]{2,1,0:T(8,128)(2,1)S(1)}, u32[]{:S(2)}, u32[]{:S(2)}) collective-permute-start(bf16[1,88,1408]{2,1,0:T(8,128)(2,1)S(1)} %get-tuple-element.34), channel_id=1, source_target_pairs={{64,0},{65,1},{66,2},{67,3},{68,128},{69,129},{70,130},{71,131},{7... | collective-permute-start | bytes 743432 | tf_op jit(solution)/shard_map/ppermute | solution.py:170
  172.4 36.8 %collective-permute-start.2 = (bf16[1,88,1408]{2,1,0:T(8,128)(2,1)S(1)}, bf16[1,88,1408]{2,1,0:T(8,128)(2,1)S(1)}, u32[]{:S(2)}, u32[]{:S(2)}) collective-permute-start(bf16[1,88,1408]{2,1,0:T(8,128)(2,1)S(1)} %get-tuple-element.35), channel_id=1, source_target_pairs={{64,128},{65,129},{66,130},{67,131},{68,0},{69,1},{70,2},{71,3},{7... | collective-permute-start | bytes 743432 | tf_op jit(solution)/shard_map/ppermute | solution.py:170
  209.2 4.1 %collective-permute-start.8 = (bf16[64,8,1792]{2,1,0:T(8,128)(2,1)}, bf16[64,8,1792]{2,1,0:T(8,128)(2,1)S(1)}, u32[]{:S(2)}, u32[]{:S(2)}) collective-permute-start(bf16[64,8,1792]{2,1,0:T(8,128)(2,1)} %collective-permute-done.3.refs_0_), channel_id=1, source_target_pairs={{0,4},{4,0},{8,12},{12,8},{16,20},{20,16},{24,28},{28,24},{32,36},... | collective-permute-start | bytes 5505032 | tf_op jit(solution)/shard_map/ppermute | solution.py:220
  209.2 13.9 %collective-permute-start.5 = (bf16[64,8,1792]{2,1,0:T(8,128)(2,1)}, bf16[64,8,1792]{2,1,0:T(8,128)(2,1)S(1)}, u32[]{:S(2)}, u32[]{:S(2)}) collective-permute-start(bf16[64,8,1792]{2,1,0:T(8,128)(2,1)} %all-to-all-done.1.refs_0_.refs_2_), channel_id=1, source_target_pairs={{0,4},{4,0},{8,12},{12,8},{16,20},{20,16},{24,28},{28,24},{32,36},... | collective-permute-start | bytes 5505032 | tf_op jit(solution)/shard_map/ppermute | solution.py:220
  209.7 52.8 %collective-permute-start.11 = (bf16[64,8,1792]{2,1,0:T(8,128)(2,1)}, bf16[64,8,1792]{2,1,0:T(8,128)(2,1)S(1)}, u32[]{:S(2)}, u32[]{:S(2)}) collective-permute-start(bf16[64,8,1792]{2,1,0:T(8,128)(2,1)} %all-to-all-done.1.refs_0_.refs_2_), channel_id=1, source_target_pairs={{0,1},{1,0},{2,3},{3,2},{4,5},{5,4},{6,7},{7,6},{8,9},{9,8},{10,11... | collective-permute-start | bytes 5505032 | tf_op jit(solution)/shard_map/ppermute | solution.py:223
  211.2 58.0 %collective-permute-start.12 = (bf16[64,8,1792]{2,1,0:T(8,128)(2,1)}, bf16[64,8,1792]{2,1,0:T(8,128)(2,1)S(1)}, u32[]{:S(2)}, u32[]{:S(2)}) collective-permute-start(bf16[64,8,1792]{2,1,0:T(8,128)(2,1)} %get-tuple-element.44.refs_3_.refs_5_), channel_id=1, source_target_pairs={{0,3},{1,2},{2,1},{3,0},{4,7},{5,6},{6,5},{7,4},{8,11},{9,10},{10,... | collective-permute-start | bytes 5505032 | tf_op jit(solution)/shard_map/ppermute | solution.py:223
  218.6 43.9 %collective-permute-start.10 = (bf16[1,88,1408]{2,1,0:T(8,128)(2,1)S(1)}, bf16[1,88,1408]{2,1,0:T(8,128)(2,1)S(1)}, u32[]{:S(2)}, u32[]{:S(2)}) collective-permute-start(bf16[1,88,1408]{2,1,0:T(8,128)(2,1)S(1)} %get-tuple-element.42), channel_id=1, source_target_pairs={{64,128},{65,129},{66,130},{67,131},{68,1},{69,0},{70,3},{71,2},{7... | collective-permute-start | bytes 743432 | tf_op jit(solution)/shard_map/ppermute | solution.py:170
  221.5 41.0 %collective-permute-start.9 = (bf16[1,88,1408]{2,1,0:T(8,128)(2,1)S(1)}, bf16[1,88,1408]{2,1,0:T(8,128)(2,1)S(1)}, u32[]{:S(2)}, u32[]{:S(2)}) collective-permute-start(bf16[1,88,1408]{2,1,0:T(8,128)(2,1)S(1)} %get-tuple-element.41), channel_id=1, source_target_pairs={{64,1},{65,0},{66,3},{67,2},{68,128},{69,129},{70,130},{71,131},{7... | collective-permute-start | bytes 743432 | tf_op jit(solution)/shard_map/ppermute | solution.py:170
  223.1 6.0 %copy-start.1 = (bf16[64,8,1792]{2,1,0:T(8,128)(2,1)}, bf16[64,8,1792]{2,1,0:T(8,128)(2,1)S(1)}, u32[]{:S(2)}) copy-start(bf16[64,8,1792]{2,1,0:T(8,128)(2,1)S(1)} %collective-permute-done.5.refs_1_.refs_3_) | copy-start | bytes 5505028
  229.1 33.4 %collective-permute-start.6 = (bf16[1,88,1408]{2,1,0:T(8,128)(2,1)S(1)}, bf16[1,88,1408]{2,1,0:T(8,128)(2,1)S(1)}, u32[]{:S(2)}, u32[]{:S(2)}) collective-permute-start(bf16[1,88,1408]{2,1,0:T(8,128)(2,1)S(1)} %get-tuple-element.38), channel_id=1, source_target_pairs={{64,0},{65,1},{66,2},{67,3},{68,128},{69,129},{70,130},{71,131},{7... | collective-permute-start | bytes 743432 | tf_op jit(solution)/shard_map/ppermute | solution.py:170
  262.5 16.5 %copy-start.8 = (bf16[64,8,1792]{2,1,0:T(8,128)(2,1)}, bf16[64,8,1792]{2,1,0:T(8,128)(2,1)S(1)}, u32[]{:S(2)}) copy-start(bf16[64,8,1792]{2,1,0:T(8,128)(2,1)S(1)} %collective-permute-done.11.refs_2_) | copy-start | bytes 5505028
  262.5 6.6 %collective-permute-start.7 = (bf16[1,88,1408]{2,1,0:T(8,128)(2,1)S(1)}, bf16[1,88,1408]{2,1,0:T(8,128)(2,1)S(1)}, u32[]{:S(2)}, u32[]{:S(2)}) collective-permute-start(bf16[1,88,1408]{2,1,0:T(8,128)(2,1)S(1)} %get-tuple-element.39), channel_id=1, source_target_pairs={{64,128},{65,129},{66,130},{67,131},{68,0},{69,1},{70,2},{71,3},{7... | collective-permute-start | bytes 743432 | tf_op jit(solution)/shard_map/ppermute | solution.py:170
  269.2 19.5 %collective-permute-start.13 = (bf16[64,8,1792]{2,1,0:T(8,128)(2,1)S(1)}, bf16[64,8,1792]{2,1,0:T(8,128)(2,1)S(1)}, u32[]{:S(2)}, u32[]{:S(2)}) collective-permute-start(bf16[64,8,1792]{2,1,0:T(8,128)(2,1)S(1)} %collective-permute-done.11.refs_2_), channel_id=1, source_target_pairs={{0,4},{4,0},{8,12},{12,8},{16,20},{20,16},{24,28},{28,24},{32,36},... | collective-permute-start | bytes 5505032 | tf_op jit(solution)/shard_map/ppermute | solution.py:220
  269.2 1.3 copy-start.7
  279.0 38.5 %collective-permute-start.20 = (bf16[2,88,1408]{2,1,0:T(8,128)(2,1)S(1)}, bf16[2,88,1408]{2,1,0:T(8,128)(2,1)S(1)}, u32[]{:S(2)}, u32[]{:S(2)}) collective-permute-start(bf16[2,88,1408]{2,1,0:T(8,128)(2,1)S(1)} %get-tuple-element.46), channel_id=1, source_target_pairs={{64,0},{65,1},{66,2},{67,3},{68,131},{69,130},{70,129},{71,128},{7... | collective-permute-start | bytes 1486856 | tf_op jit(solution)/shard_map/ppermute | solution.py:170
  286.5 31.0 %collective-permute-start.21 = (bf16[2,88,1408]{2,1,0:T(8,128)(2,1)S(1)}, bf16[2,88,1408]{2,1,0:T(8,128)(2,1)S(1)}, u32[]{:S(2)}, u32[]{:S(2)}) collective-permute-start(bf16[2,88,1408]{2,1,0:T(8,128)(2,1)S(1)} %get-tuple-element.47), channel_id=1, source_target_pairs={{64,131},{65,130},{66,129},{67,128},{68,0},{69,1},{70,2},{71,3},{7... | collective-permute-start | bytes 1486856 | tf_op jit(solution)/shard_map/ppermute | solution.py:170
  288.7 1.2 copy-start.9
  302.0 21.4 %collective-permute-start.14 = (bf16[1,88,1408]{2,1,0:T(8,128)(2,1)S(1)}, bf16[1,88,1408]{2,1,0:T(8,128)(2,1)S(1)}, u32[]{:S(2)}, u32[]{:S(2)}) collective-permute-start(bf16[1,88,1408]{2,1,0:T(8,128)(2,1)S(1)} %get-tuple-element.49), channel_id=1, source_target_pairs={{64,1},{65,0},{66,3},{67,2},{68,128},{69,129},{70,130},{71,131},{7... | collective-permute-start | bytes 743432 | tf_op jit(solution)/shard_map/ppermute | solution.py:170
  303.3 25.2 %collective-permute-start.15 = (bf16[1,88,1408]{2,1,0:T(8,128)(2,1)}, bf16[1,88,1408]{2,1,0:T(8,128)(2,1)}, u32[]{:S(2)}, u32[]{:S(2)}) collective-permute-start(bf16[1,88,1408]{2,1,0:T(8,128)(2,1)} %get-tuple-element.50), channel_id=1, source_target_pairs={{64,128},{65,129},{66,130},{67,131},{68,1},{69,0},{70,3},{71,2},{7... | collective-permute-start | bytes 743432 | tf_op jit(solution)/shard_map/ppermute | solution.py:170
  303.5 25.1 %collective-permute-start.16 = (bf16[1,88,1408]{2,1,0:T(8,128)(2,1)}, bf16[1,88,1408]{2,1,0:T(8,128)(2,1)}, u32[]{:S(2)}, u32[]{:S(2)}) collective-permute-start(bf16[1,88,1408]{2,1,0:T(8,128)(2,1)} %get-tuple-element.51), channel_id=1, source_target_pairs={{64,1},{65,0},{66,3},{67,2},{68,131},{69,130},{70,129},{71,128},{7... | collective-permute-start | bytes 743432 | tf_op jit(solution)/shard_map/ppermute | solution.py:170
  317.5 20.3 %collective-permute-start.17 = (bf16[1,88,1408]{2,1,0:T(8,128)(2,1)}, bf16[1,88,1408]{2,1,0:T(8,128)(2,1)}, u32[]{:S(2)}, u32[]{:S(2)}) collective-permute-start(bf16[1,88,1408]{2,1,0:T(8,128)(2,1)} %get-tuple-element.52), channel_id=1, source_target_pairs={{64,131},{65,130},{66,129},{67,128},{68,1},{69,0},{70,3},{71,2},{7... | collective-permute-start | bytes 743432 | tf_op jit(solution)/shard_map/ppermute | solution.py:170
  317.5 21.9 %collective-permute-start.18 = (bf16[1,88,1408]{2,1,0:T(8,128)(2,1)}, bf16[1,88,1408]{2,1,0:T(8,128)(2,1)}, u32[]{:S(2)}, u32[]{:S(2)}) collective-permute-start(bf16[1,88,1408]{2,1,0:T(8,128)(2,1)} %get-tuple-element.53), channel_id=1, source_target_pairs={{64,1},{65,0},{66,3},{67,2},{68,131},{69,130},{70,129},{71,128},{7... | collective-permute-start | bytes 743432 | tf_op jit(solution)/shard_map/ppermute | solution.py:170
  323.3 0.7 copy-start.4
  324.0 18.7 %collective-permute-start.19 = (bf16[1,88,1408]{2,1,0:T(8,128)(2,1)}, bf16[1,88,1408]{2,1,0:T(8,128)(2,1)}, u32[]{:S(2)}, u32[]{:S(2)}) collective-permute-start(bf16[1,88,1408]{2,1,0:T(8,128)(2,1)} %get-tuple-element.54), channel_id=1, source_target_pairs={{64,131},{65,130},{66,129},{67,128},{68,1},{69,0},{70,3},{71,2},{7... | collective-permute-start | bytes 743432 | tf_op jit(solution)/shard_map/ppermute | solution.py:170
  342.7 0.9 copy-start.5

commit v3 on v2

--- a/solution.py
+++ b/solution.py
@@ -56,24 +56,23 @@
     return cut + ([(slice(whole, quarter), slice(start, start + rest))] if rest else [])
 
 
-def pack_body(m_lanes, l_ref, x_ref, one_ref, two_ref):
+def pack_body(l_ref, x_ref, m_ref, *k_refs):
     quarter = l_ref.shape[1]
-    spots = one_ref.shape[0]
+    spots, half = m_ref.shape[0], m_ref.shape[-1] // 2
     turned = []
     for ref in (l_ref, x_ref):
         block = jnp.swapaxes(jnp.swapaxes(ref[...].astype(jnp.float32), 1, 2), 0, 1)
         turned.append(block.astype(jnp.bfloat16).reshape(2, spots, 2, SUB, quarter))
     step = pl.program_id(0)
-    n_groups = two_ref.shape[-1] // quarter
-    starts = (0, m_lanes // 2, m_lanes)
+    n_groups = half // quarter
     for at in range(n_groups):
 
         @pl.when(step == at)
         def _():
             for r in range(2):
-                blocks = (turned[1 - r][1, :, r], turned[r][1, :, r], turned[r][0, :, 0], turned[r][0, :, 1])
-                spots_of = [(one_ref, start) for start in starts] + [(two_ref, 0)]
-                for block, (ref, start) in zip(blocks, spots_of):
+                places = [(turned[1 - r][1, :, r], m_ref, 0), (turned[r][1, :, r], m_ref, half)]
+                places += [(turned[r][0, :, i], k_ref, 0) for i, k_ref in enumerate(k_refs)]
+                for block, ref, start in places:
                     for of, to in pieces(quarter, n_groups, at):
                         ref[:, r, :, start + to.start : start + to.stop] = block[:, :, of]
 
@@ -81,11 +80,10 @@
 def pack(chol, dressed):
     rows, quarter, orbitals = chol.shape
     spots, groups = orbitals // 4, rows // SUB
-    k_lanes = ceil_lanes(groups * quarter)
-    m_lanes = 2 * k_lanes
-    shapes = [(spots, 2, SUB, m_lanes + k_lanes), (spots, 2, SUB, k_lanes)]
-    one, two = pl.pallas_call(
-        functools.partial(pack_body, m_lanes),
+    lanes = ceil_lanes(groups * quarter)
+    shapes = [(spots, 2, SUB, wide) for wide in (2 * lanes, lanes, lanes)]
+    out = pl.pallas_call(
+        pack_body,
         grid=(groups,),
         in_specs=[pl.BlockSpec((SUB, quarter, orbitals), lambda n: (n, 0, 0))] * 2,
         out_specs=[pl.BlockSpec(shape, lambda n: (0, 0, 0, 0)) for shape in shapes],
@@ -93,7 +91,7 @@
         compiler_params=PARAMS,
         name="pack",
     )(chol, dressed)
-    return one.reshape(-1, SUB, m_lanes + k_lanes), two.reshape(-1, SUB, k_lanes), k_lanes
+    return [a.reshape(2 * spots, SUB, a.shape[-1]) for a in out], lanes
 
 
 def in_lanes(ref, tile):
@@ -147,15 +145,16 @@
 
 
 def tiles(name, quarter, core, lefts, rights, messages):
-    arrays = [a for pair in (*lefts, *rights) for a in pair]
-    width = arrays[0].shape[0]
-    groups = arrays[0].shape[-1] // quarter
+    ops = [op if isinstance(op, tuple) else (op, 0) for pair in (*lefts, *rights) for op in pair]
+    arrays = [array for array, _ in ops]
+    width, _, lanes = arrays[0].shape
+    groups = lanes // quarter
     shapes = [(len(message), quarter // 4, 4 * quarter) for message in messages] * 2
     out = pl.pallas_call(
         functools.partial(tiles_body, len(lefts), len(rights), messages, quarter, groups),
         grid=(width // SHARE,),
         in_specs=[pl.BlockSpec(memory_space=pltpu.SMEM)]
-        + [pl.BlockSpec((SHARE, *a.shape[1:]), lambda n: (n, 0, 0)) for a in arrays],
+        + [pl.BlockSpec((SHARE, SUB, lanes), lambda n, half=half: (n, 0, half)) for _, half in ops],
         out_specs=[pl.BlockSpec(shape, lambda n: (0, 0, 0)) for shape in shapes],
         out_shape=[jax.ShapeDtypeStruct(shape, jnp.bfloat16) for shape in shapes],
         scratch_shapes=[pltpu.VMEM((sum(map(len, messages)), quarter, quarter), jnp.float32)],
@@ -171,7 +170,7 @@
     ]
 
 
-def home_body(spots, where_ref, pairs_ref, mask_ref, *refs):
+def home_body(index, where_ref, pairs_ref, mask_ref, *refs):
     arrived, out_ref, held = refs[:-2], refs[-2], refs[-1]
     is_k, g = where_ref[0], where_ref[1]
     u, v = pl.program_id(0), pl.program_id(1)
@@ -185,9 +184,8 @@
             @pl.when((use == at) & (i == orbital))
             def _():
                 for bits in range(4):
-                    ref, index = spots[bits, orbital]
-                    ref = arrived[2 * ref + at]
-                    parts = [ref[index, :, n * quarter : (n + 1) * quarter].astype(jnp.float32) for n in range(4)]
+                    ref = arrived[2 * (4 * orbital + bits) + at]
+                    parts = [ref[index[bits, orbital], :, n * quarter : (n + 1) * quarter].astype(jnp.float32) for n in range(4)]
                     held[bits] = jnp.concatenate(parts, axis=0).astype(jnp.bfloat16)
 
     for q in range(4):
@@ -195,11 +193,11 @@
         out_ref[0, 0, :, lanes] = held[q ^ g] * (mask_ref[:, lanes] * scale)
 
 
-def home(spots, where, pairs, mask, arrays):
+def home(index, where, pairs, mask, arrays):
     quarter, whole = mask.shape
     full = [pl.BlockSpec(a.shape, lambda u, v, k=a.ndim: (0,) * k) for a in (mask, *arrays)]
     return pl.pallas_call(
-        functools.partial(home_body, spots),
+        functools.partial(home_body, index),
         grid=(2, 2),
         in_specs=[pl.BlockSpec(memory_space=pltpu.SMEM)] * 2 + full,
         out_specs=pl.BlockSpec((1, 1, quarter, whole), lambda u, v: (u, v, 0, 0)),
@@ -225,39 +223,41 @@
     def after(value, *others):
         return lax.optimization_barrier((value, *others))[0]
 
-    one, two, lanes = pack(*[jnp.transpose(a, (0, 2, 1)) for a in (chol, dressed)])
-    one = lax.all_to_all(one, "occ", 0, 0, axis_index_groups=order, tiled=True)
-    m_own = one[:, :, :lanes]
-    one, two, m_own = lax.optimization_barrier((one, two, m_own))
-    m_far, k0 = one[:, :, lanes : 2 * lanes], one[:, :, 2 * lanes :]
-    k1 = lax.all_to_all(two, "occ", 0, 0, axis_index_groups=order, tiled=True)
-
-    m_own_x = across(m_own, 3)
-    near0, far0 = (k0, to_core(k0)), across(k0, 1)
-    m = (m_own, m_far)
-    (oo0,) = tiles("first", quarter, core, [near0], [m], [[(0, 0)]])
-    got_oo0 = send(oo0, 0, 0)
-
-    far0, k1, m_far = lax.optimization_barrier((far0, k1, m_far, m_own_x, *got_oo0))[:3]
-    m_x = (m_own_x, across(m_far, 3))
-    near1, far1 = (k1, to_core(k1)), across(k1, 1)
-    far0 = (far0, to_core(far0))
-    (po0,) = tiles("early", quarter, core, [far0], [m], [[(0, 0)]])
-    got_po0 = send(po0, 1, 0)
-    (oo1,) = tiles("near", quarter, core, [near1], [m], [[(0, 0)]])
-    got_oo1 = send(oo1, 0, 0)
-
-    far1 = after(far1, *got_po0, *got_oo1)
-    far1 = (far1, to_core(far1))
-    m_x = (m_x[0], after(m_x[1], *got_po0, *got_oo1))
-    (op,) = tiles("middle", quarter, core, [near0, near1], [m_x], [[(0, 0), (1, 0)]])
-    got_op = send(op, 0, 3)
-    far1 = (after(far1[0], *op), far1[1])
-    pp0, po1, pp1 = tiles("late", quarter, core, [far0, far1], [m, m_x], [[(0, 1)], [(1, 0)], [(1, 1)]])
-    got_pp0, got_po1, got_pp1 = send(pp0, 1, 3), send(po1, 1, 0), send(pp1, 1, 3)
-    arrived = [*got_oo0, *got_oo1, *got_po0, *got_po1, *got_pp0, *got_pp1, *got_op]
-    spots = {(bits, i): (2 * bits + i, 0) for bits in range(3) for i in range(2)}
-    spots |= {(3, i): (6, i) for i in range(2)}
+    def centre(part):
+        return lax.all_to_all(part, "occ", 0, 0, axis_index_groups=order, tiled=True)
+
+    (m, k0, k1), lanes = pack(*[jnp.transpose(a, (0, 2, 1)) for a in (chol, dressed)])
+    m, k0, k1 = centre(m), centre(k0), centre(k1)
+
+    m_1, m_3 = across(m, 1), across(m, 3)
+    k0 = (k0, to_core(k0))
+    ms = {0: ((m, 0), (m, 1))}
+    got = {}
+
+    def compute(name, ks, spots):
+        messages = [[(left, right) for left in range(len(ks))] for right in range(len(spots))]
+        return tiles(name, quarter, core, ks, [ms[q] for q in spots], messages)
+
+    first = compute("first", [k0], [0])
+    got[0, 0] = send(first[0], 0, 0)
+    m_1, m_3 = lax.optimization_barrier((m_1, m_3, *first[0]))[:2]
+    ms |= {1: ((m_1, 0), (m_1, 1)), 3: ((m_3, 0), (m_3, 1))}
+    m_2 = m_3[:, :, :lanes], m_1[:, :, lanes:]
+    k0_own, *m_2 = lax.optimization_barrier((k0[0], *m_2))
+    m_2 = across(m_2[0], 1), across(m_2[1], 3)
+    k0 = (k0_own, k0[1])
+    second = compute("second", [k0], [1, 3])
+    got[1, 0], got[3, 0] = send(second[0], 0, 1), send(second[1], 0, 3)
+    k1 = after(k1, *second[0])
+    k1 = (k1, to_core(k1))
+    third = compute("third", [k1], [0, 1, 3])
+    for q, message in zip((0, 1, 3), third):
+        got[q, 1] = send(message, 0, q)
+    ms[2] = lax.optimization_barrier((*m_2, *got[0, 0], *got[1, 0], *got[3, 0], *got[0, 1]))[:2]
+    fourth = compute("fourth", [k0, k1], [2])
+    got[2, 0] = got[2, 1] = send(fourth[0], 0, 2)
+    arrived = [a for i in range(2) for q in range(4) for a in got[q, i]]
+    index = {(q, i): i if q == 2 else 0 for q in range(4) for i in range(2)}
 
     mirror = (occ + PLACES // 2) % PLACES
     pairs = lax.dynamic_slice(pair_mask, (occ * 2, mirror * 2), (2, 2))
@@ -265,7 +265,7 @@
     sym_rows = lax.dynamic_slice_in_dim(sym_mask, g * rows_per, rows_per, 0)
     mask = jnp.repeat(jnp.repeat(sym_rows.astype(jnp.bfloat16), SLAB, 0), SLAB, 1)
     where = jnp.stack([(occ < PLACES // 2).astype(jnp.int32), g.astype(jnp.int32)])
-    return home(spots, where, pairs, mask, arrived)
+    return home(index, where, pairs, mask, arrived)
 
 
 def solution(mesh):

time: 354 us -> 335 us (0.946)
  blocking collectives: 136 us -> 97 us
  waiting for transfers between devices: 98.4 us -> 121 us
    ppermute x4, waiting for transfers between devices: 64 us -> 22.9 us  [across(): return lax.ppermute(part, 'vir', x_route(bits))]
    all_to_all x1 -> x2, waiting for transfers between devices: 0.01 us -> 40.9 us  [centre(): lax.all_to_all(part, 'occ', 0, 0, axis_index_groups=order, tiled=True)]
    all_to_all x1, blocking collectives: 136 us -> 97 us  [centre(): lax.all_to_all(part, 'occ', 0, 0, axis_index_groups=order, tiled=True)]
    ppermute x14, waiting for transfers between devices: 33.4 us -> 53.5 us  [send(): lax.ppermute(pair[at], ('occ', 'vir'), home_route(at == 0, k_bits, m_bits))]
    all_to_all x1 -> x2, starting transfers between devices: 7.33 us -> 14.1 us  [centre(): lax.all_to_all(part, 'occ', 0, 0, axis_index_groups=order, tiled=True)]
    unnamed x20 -> x26, local copies, waits for them, and re-layouts: 8.52 us -> 5.67 us
    pallas_call x5 -> x4, Pallas kernels: 37.5 us -> 35.8 us  [tiles(): pl.pallas_call(functools.partial(tiles_body, len(lefts), len(rights), mes...]
  transfers between devices with their start and end apart: 23 -> 22, of which waited for: 12 -> 12; matrix products, arithmetic and copies ran while one was open for 2% -> 3% of each run, Pallas kernels for 11% -> 11%
where the time goes in v3:
time: 335 us; the launch traced here: 333 us
  waiting for transfers between devices  121 us (36%)
  blocking collectives  97 us (29%)
  Pallas kernels  52.1 us (16%)
  starting transfers between devices  46.9 us (14%)
  local copies, waits for them, and re-layouts  15 us (4%)
    all_to_all x1, blocking collectives, centre(): lax.all_to_all(part, 'occ', 0, 0, axis_index_groups=order, tiled=True)  97 us
    ppermute x14, waiting for transfers between devices, send(): lax.ppermute(pair[at], ('occ', 'vir'), home_route(at == 0, k_bits, m_bits))  53.5 us
    all_to_all x2, waiting for transfers between devices, centre(): lax.all_to_all(part, 'occ', 0, 0, axis_index_groups=order, tiled=True)  40.9 us
    pallas_call x4, Pallas kernels, tiles(): pl.pallas_call(functools.partial(tiles_body, len(lefts), len(rights), mes...  35.8 us
    ppermute x14, starting transfers between devices, send(): lax.ppermute(pair[at], ('occ', 'vir'), home_route(at == 0, k_bits, m_bits))  26.6 us
    ppermute x4, waiting for transfers between devices, across(): return lax.ppermute(part, 'vir', x_route(bits))  22.9 us
    all_to_all x2, starting transfers between devices, centre(): lax.all_to_all(part, 'occ', 0, 0, axis_index_groups=order, tiled=True)  14.1 us
    pallas_call x1, Pallas kernels, pack(): pl.pallas_call(pack_body, grid=(groups,), in_specs=[pl.BlockSpec((SUB, qu...  10.1 us
  transfers between devices with their start and end apart: 22, of which 12 were waited for; matrix products, arithmetic and copies ran while one was open for 3% of the time, Pallas kernels for 11%

profile of v3, /device:TPU:8, one launch (start us, length us, event | category | flops | bytes accessed | tf_op | source)
XLA Modules:
  0.0 333.0 jit_solution(5943092030811631048)
XLA Ops:
  0.0 10.1 %pack.1 = (bf16[32,2,8,3584]{3,2,1,0:T(8,128)(2,1)}, bf16[32,2,8,1792]{3,2,1,0:T(8,128)(2,1)S(1)}, bf16[32,2,8,1792]{3,2,1,0:T(8,128)(2,1)S(1)}) custom-call(bf16[40,352,128]{2,1,0:T(8,128)(2,1)} %bitcast.14, bf16[40,352,128]{2,1,0:T(8,128)(2,1)} %bitcast.15), custom_call_target="tpu_custom_call" | custom-call | tf_op jit(solution)/shard_map/pack/pallas_call | solution.py:85
  10.1 97.0 %all_to_all.15.refs_2_.refs_3_ = bf16[64,8,3584]{2,1,0:T(8,128)(2,1)} all-to-all(bf16[64,8,3584]{2,1,0:T(8,128)(2,1)} %bitcast.13), channel_id=1, replica_groups={{64,68,192,196,72,76,200,204,80,84,208,212,88,92,216,220,96,100,224,228..., dimensions={0} | all-to-all | bytes 7340032 | tf_op jit(solution)/shard_map/all_to_all | solution.py:227
  107.1 7.0 %all-to-all-start = ((bf16[64,8,1792]{2,1,0:T(8,128)(2,1)}), bf16[64,8,1792]{2,1,0:T(8,128)(2,1)S(1)}, u32[]{:S(2)}, u32[]{:S(2)}) async-start(bf16[64,8,1792]{2,1,0:T(8,128)(2,1)} %bitcast.11), calls=%async_computation | async-start | bytes 3670016 | tf_op jit(solution)/shard_map/all_to_all | solution.py:227
  114.1 1.6 collective-permute-start.3
  115.7 2.1 collective-permute-start.4
  117.8 40.9 %all-to-all-done.refs_0_ = bf16[64,8,1792]{2,1,0:T(8,128)(2,1)S(1)} async-done(((bf16[64,8,1792]{2,1,0:T(8,128)(2,1)}), bf16[64,8,1792]{2,1,0:T(8,128)(2,1)S(1)}, u32[]{:S(2)}, u32[]{:S(2)}) %all-to-all-start) | async-done | bytes 1835040 | tf_op jit(solution)/shard_map/all_to_all | solution.py:227
  158.7 7.1 %all-to-all-start.2 = ((bf16[64,8,1792]{2,1,0:T(8,128)(2,1)}), bf16[64,8,1792]{2,1,0:T(8,128)(2,1)}, u32[]{:S(2)}, u32[]{:S(2)}) async-start(bf16[64,8,1792]{2,1,0:T(8,128)(2,1)} %bitcast.10), calls=%async_computation.2 | async-start | bytes 3670016 | tf_op jit(solution)/shard_map/all_to_all | solution.py:227
  165.8 0.2 collective-permute-start
  166.0 3.8 %collective-permute-done.refs_1_ = bf16[64,8,1792]{2,1,0:T(8,128)(2,1)} collective-permute-done((bf16[64,8,1792]{2,1,0:T(8,128)(2,1)S(1)}, bf16[64,8,1792]{2,1,0:T(8,128)(2,1)}, u32[]{:S(2)}, u32[]{:S(2)}) %collective-permute-start) | collective-permute-done | bytes 1835040 | tf_op jit(solution)/shard_map/ppermute | solution.py:218
  169.8 5.7 %first.1 = (bf16[1,88,1408]{2,1,0:T(8,128)(2,1)S(1)}, bf16[1,88,1408]{2,1,0:T(8,128)(2,1)S(1)}) custom-call(s32[1]{0:T(128)} %bitcast.4.core_ref, bf16[64,8,1792]{2,1,0:T(8,128)(2,1)S(1)} %all-to-all-done.refs_0_, bf16[64,8,1792]{2,1,0:T(8,128)(2,1)} %collective-permute-done.refs_1_, bf16[64,8,3584]{2,1,0:T(8,128)(2,1)} %all_to_all.15.refs_2_.refs_3_, ...), custom_call_target="tpu_custom_call" | custom-call | tf_op jit(solution)/shard_map/first/pallas_call | solution.py:153
  175.5 20.4 %collective-permute-done.3.refs_2_.refs_3_.refs_4_.refs_5_ = bf16[64,8,3584]{2,1,0:T(8,128)(2,1)} collective-permute-done((bf16[64,8,3584]{2,1,0:T(8,128)(2,1)}, bf16[64,8,3584]{2,1,0:T(8,128)(2,1)}, u32[]{:S(2)}, u32[]{:S(2)}) %collective-permute-start.3) | collective-permute-done | bytes 3670048 | tf_op jit(solution)/shard_map/ppermute | solution.py:221
  195.9 2.4 collective-permute-done.4.refs_4_.refs_5_.refs_6_.refs_7_
  198.3 2.9 slice.6
  201.2 2.9 slice.7
  204.1 8.9 %second.1 = (bf16[1,88,1408]{2,1,0:T(8,128)(2,1)}, bf16[1,88,1408]{2,1,0:T(8,128)(2,1)S(1)}, bf16[1,88,1408]{2,1,0:T(8,128)(2,1)S(1)}, bf16[1,88,1408]{2,1,0:T(8,128)(2,1)}) custom-call(s32[1]{0:T(128)} %bitcast.4.core_ref, bf16[64,8,1792]{2,1,0:T(8,128)(2,1)S(1)} %all-to-all-done.refs_0_, bf16[64,8,1792]{2,1,0:T(8,128)(2,1)} %collective-permute-done.refs_1_, ...), custom_call_target="tpu_custom_call" | custom-call | tf_op jit(solution)/shard_map/second/pallas_call | solution.py:153
  213.0 0.7 copy-done.9
  213.7 0.0 all-to-all-done.2.refs_0_.refs_2_
  213.7 0.0 collective-permute-start.7
  213.7 0.0 collective-permute-start.8
  213.7 2.4 collective-permute-start.9
  216.1 0.0 collective-permute-start.1
  216.1 3.4 %collective-permute-start.2 = (bf16[1,88,1408]{2,1,0:T(8,128)(2,1)S(1)}, bf16[1,88,1408]{2,1,0:T(8,128)(2,1)S(1)}, u32[]{:S(2)}, u32[]{:S(2)}) collective-permute-start(bf16[1,88,1408]{2,1,0:T(8,128)(2,1)S(1)} %get-tuple-element.33), channel_id=1, source_target_pairs={{64,128},{65,129},{66,130},{67,131},{68,0},{69,1},{70,2},{71,3},{7... | collective-permute-start | bytes 743432 | tf_op jit(solution)/shard_map/ppermute | solution.py:169
  219.5 11.5 %collective-permute-done.1.refs_0_ = bf16[1,88,1408]{2,1,0:T(8,128)(2,1)S(1)} collective-permute-done((bf16[1,88,1408]{2,1,0:T(8,128)(2,1)S(1)}, bf16[1,88,1408]{2,1,0:T(8,128)(2,1)S(1)}, u32[]{:S(2)}, u32[]{:S(2)}) %collective-permute-start.1) | collective-permute-done | bytes 247840 | tf_op jit(solution)/shard_map/ppermute | solution.py:169
  231.0 0.0 collective-permute-start.10
  231.0 0.2 collective-permute-done.2.refs_1_
  231.2 3.6 %collective-permute-start.11 = (bf16[1,88,1408]{2,1,0:T(8,128)(2,1)}, bf16[1,88,1408]{2,1,0:T(8,128)(2,1)S(1)}, u32[]{:S(2)}, u32[]{:S(2)}) collective-permute-start(bf16[1,88,1408]{2,1,0:T(8,128)(2,1)} %get-tuple-element.44), channel_id=1, source_target_pairs={{64,131},{65,130},{66,129},{67,128},{68,0},{69,1},{70,2},{71,3},{7... | collective-permute-start | bytes 743432 | tf_op jit(solution)/shard_map/ppermute | solution.py:169
  234.8 0.0 collective-permute-done.7.refs_1_.refs_3_
  234.8 0.0 collective-permute-start.5
  234.8 12.0 %third.1 = (bf16[1,88,1408]{2,1,0:T(8,128)(2,1)S(1)}, bf16[1,88,1408]{2,1,0:T(8,128)(2,1)S(1)}, bf16[1,88,1408]{2,1,0:T(8,128)(2,1)}, bf16[1,88,1408]{2,1,0:T(8,...) custom-call(s32[1]{0:T(128)} %bitcast.4.core_ref, ...), custom_call_target="tpu_custom_call" | custom-call | tf_op jit(solution)/shard_map/third/pallas_call | solution.py:153
  246.8 0.2 collective-permute-done.10.refs_6_
  247.0 3.6 %collective-permute-start.6 = (bf16[1,88,1408]{2,1,0:T(8,128)(2,1)S(1)}, bf16[1,88,1408]{2,1,0:T(8,128)(2,1)S(1)}, u32[]{:S(2)}, u32[]{:S(2)}) collective-permute-start(bf16[1,88,1408]{2,1,0:T(8,128)(2,1)S(1)} %copy-done.10), channel_id=1, source_target_pairs={{64,129},{65,128},{66,131},{67,130},{68,0},{69,1},{70,2},{71,3},{7... | collective-permute-start | bytes 743432 | tf_op jit(solution)/shard_map/ppermute | solution.py:169
  250.6 0.0 collective-permute-done.11.refs_7_
  250.6 0.0 collective-permute-start.12
  250.6 0.0 collective-permute-done.5.refs_2_
  250.6 2.6 collective-permute-start.13
  253.3 10.8 %collective-permute-done.6.refs_3_ = bf16[1,88,1408]{2,1,0:T(8,128)(2,1)S(1)} collective-permute-done((bf16[1,88,1408]{2,1,0:T(8,128)(2,1)S(1)}, bf16[1,88,1408]{2,1,0:T(8,128)(2,1)S(1)}, u32[]{:S(2)}, u32[]{:S(2)}) %collective-permute-start.6) | collective-permute-done | bytes 247840 | tf_op jit(solution)/shard_map/ppermute | solution.py:169
  264.1 0.0 collective-permute-start.16
  264.1 0.0 collective-permute-done.8.refs_4_
  264.1 0.0 collective-permute-done.9.refs_5_
  264.1 3.3 collective-permute-done.12.refs_8_
  267.4 0.7 copy-done.3
  268.1 0.4 collective-permute-done.13.refs_9_
  268.5 0.7 copy-done.5
  269.2 9.2 %fourth.1 = (bf16[2,88,1408]{2,1,0:T(8,128)(2,1)}, bf16[2,88,1408]{2,1,0:T(8,128)(2,1)}) custom-call(s32[1]{0:T(128)} %bitcast.4.core_ref, bf16[64,8,1792]{2,1,0:T(8,128)(2,1)S(1)} %all-to-all-done.refs_0_, bf16[64,8,1792]{2,1,0:T(8,128)(2,1)} %collective-permute-done.refs_1_, bf16[64,8,1792]{2,1,0:T(8,128)(2,1)} %all-to-all-done.2.refs_0_.refs_2_, ...), custom_call_target="tpu_custom_call" | custom-call | tf_op jit(solution)/shard_map/fourth/pallas_call | solution.py:153
  278.4 1.1 collective-permute-start.14
  279.5 6.8 %collective-permute-start.15 = (bf16[2,88,1408]{2,1,0:T(8,128)(2,1)}, bf16[2,88,1408]{2,1,0:T(8,128)(2,1)S(1)}, u32[]{:S(2)}, u32[]{:S(2)}) collective-permute-start(bf16[2,88,1408]{2,1,0:T(8,128)(2,1)} %get-tuple-element.50), channel_id=1, source_target_pairs={{64,130},{65,131},{66,128},{67,129},{68,0},{69,1},{70,2},{71,3},{7... | collective-permute-start | bytes 1486856 | tf_op jit(solution)/shard_map/ppermute | solution.py:169
  286.3 2.9 collective-permute-start.17
  289.2 0.0 collective-permute-done.16.refs_10_
  289.2 0.7 copy-done.7
  289.9 2.5 collective-permute-start.19
  292.4 0.7 dynamic-slice_convert_fusion
  293.2 0.1 copy.7
  293.3 1.1 broadcast_in_dim.7
  294.4 1.7 copy.8.mask_ref
  296.1 0.8 dynamic_slice.6.pairs_ref
  296.8 0.1 pad_add_fusion.where_ref
  296.9 20.9 %collective-permute-done.17.refs_11_ = bf16[1,88,1408]{2,1,0:T(8,128)(2,1)} collective-permute-done((bf16[1,88,1408]{2,1,0:T(8,128)(2,1)}, bf16[1,88,1408]{2,1,0:T(8,128)(2,1)}, u32[]{:S(2)}, u32[]{:S(2)}) %collective-permute-start.17) | collective-permute-done | bytes 247840 | tf_op jit(solution)/shard_map/ppermute | solution.py:169
  317.8 6.2 %collective-permute-done.19.refs_15_ = bf16[1,88,1408]{2,1,0:T(8,128)(2,1)} collective-permute-done((bf16[1,88,1408]{2,1,0:T(8,128)(2,1)}, bf16[1,88,1408]{2,1,0:T(8,128)(2,1)}, u32[]{:S(2)}, u32[]{:S(2)}) %collective-permute-start.19) | collective-permute-done | bytes 247840 | tf_op jit(solution)/shard_map/ppermute | solution.py:169
  324.0 0.0 collective-permute-done.14.refs_4_.refs_12_
  324.0 0.0 collective-permute-done.15.refs_5_.refs_13_
  324.0 0.9 copy-done.4
  324.9 0.9 copy-done.6
  325.9 0.9 copy-done.8
  326.8 6.2 %home.1 = bf16[2,2,352,1408]{3,2,1,0:T(8,128)(2,1)} custom-call(s32[2]{0:T(128)S(1)} %pad_add_fusion.where_ref, s32[2,2]{1,0:T(2,128)S(1)} %dynamic_slice.6.pairs_ref, bf16[352,1408]{1,0:T(8,128)(2,1)S(1)} %copy.8.mask_ref, bf16[1,88,1408]{2,1,0:T(8,128)(2,1)S(1)} %collective-permute-done.1.refs_0_, bf16[1,88,1408]{2,1,0:T(8,128)(2,1)S(1)} %collective-permute-done.2.refs_1_, ...), custom_call_target="tpu_custom_call" | custom-call | tf_op jit(solution)/shard_map/home/pallas_call | solution.py:199
  (22 shorter events, 0.1 us)
Async XLA Ops:
  10.1 97.0 %copy-start.1 = (bf16[32,2,8,1792]{3,2,1,0:T(8,128)(2,1)}, bf16[32,2,8,1792]{3,2,1,0:T(8,128)(2,1)S(1)}, u32[]{:S(2)}) copy-start(bf16[32,2,8,1792]{3,2,1,0:T(8,128)(2,1)S(1)} %get-tuple-element.39) | copy-start | bytes 5505028
  10.1 97.0 %copy-start.2 = (bf16[32,2,8,1792]{3,2,1,0:T(8,128)(2,1)}, bf16[32,2,8,1792]{3,2,1,0:T(8,128)(2,1)S(1)}, u32[]{:S(2)}) copy-start(bf16[32,2,8,1792]{3,2,1,0:T(8,128)(2,1)S(1)} %get-tuple-element.30) | copy-start | bytes 5505028
  107.1 51.6 %all-to-all-start = ((bf16[64,8,1792]{2,1,0:T(8,128)(2,1)}), bf16[64,8,1792]{2,1,0:T(8,128)(2,1)S(1)}, u32[]{:S(2)}, u32[]{:S(2)}) async-start(bf16[64,8,1792]{2,1,0:T(8,128)(2,1)} %bitcast.11), calls=%async_computation | async-start | bytes 3670016 | tf_op jit(solution)/shard_map/all_to_all | solution.py:227
  114.1 81.8 %collective-permute-start.3 = (bf16[64,8,3584]{2,1,0:T(8,128)(2,1)}, bf16[64,8,3584]{2,1,0:T(8,128)(2,1)}, u32[]{:S(2)}, u32[]{:S(2)}) collective-permute-start(bf16[64,8,3584]{2,1,0:T(8,128)(2,1)} %all_to_all.15.refs_2_.refs_3_), channel_id=1, source_target_pairs={{0,1},{1,0},{2,3},{3,2},{4,5},{5,4},{6,7},{7,6},{8,9},{9,8},{10,11... | collective-permute-start | bytes 11010056 | tf_op jit(solution)/shard_map/ppermute | solution.py:221
  115.7 82.6 %collective-permute-start.4 = (bf16[64,8,3584]{2,1,0:T(8,128)(2,1)}, bf16[64,8,3584]{2,1,0:T(8,128)(2,1)}, u32[]{:S(2)}, u32[]{:S(2)}) collective-permute-start(bf16[64,8,3584]{2,1,0:T(8,128)(2,1)} %all_to_all.15.refs_2_.refs_3_), channel_id=1, source_target_pairs={{0,3},{1,2},{2,1},{3,0},{4,7},{5,6},{6,5},{7,4},{8,11},{9,10},{10,... | collective-permute-start | bytes 11010056 | tf_op jit(solution)/shard_map/ppermute | solution.py:221
  158.7 55.0 %all-to-all-start.2 = ((bf16[64,8,1792]{2,1,0:T(8,128)(2,1)}), bf16[64,8,1792]{2,1,0:T(8,128)(2,1)}, u32[]{:S(2)}, u32[]{:S(2)}) async-start(bf16[64,8,1792]{2,1,0:T(8,128)(2,1)} %bitcast.10), calls=%async_computation.2 | async-start | bytes 3670016 | tf_op jit(solution)/shard_map/all_to_all | solution.py:227
  165.8 4.0 %collective-permute-start = (bf16[64,8,1792]{2,1,0:T(8,128)(2,1)S(1)}, bf16[64,8,1792]{2,1,0:T(8,128)(2,1)}, u32[]{:S(2)}, u32[]{:S(2)}) collective-permute-start(bf16[64,8,1792]{2,1,0:T(8,128)(2,1)S(1)} %all-to-all-done.refs_0_), channel_id=1, source_target_pairs={{0,4},{4,0},{8,12},{12,8},{16,20},{20,16},{24,28},{28,24},{32,36},... | collective-permute-start | bytes 5505032 | tf_op jit(solution)/shard_map/ppermute | solution.py:218
  213.0 0.7 copy-start.9
  213.7 21.1 %collective-permute-start.7 = (bf16[64,8,1792]{2,1,0:T(8,128)(2,1)}, bf16[64,8,1792]{2,1,0:T(8,128)(2,1)S(1)}, u32[]{:S(2)}, u32[]{:S(2)}) collective-permute-start(bf16[64,8,1792]{2,1,0:T(8,128)(2,1)} %all-to-all-done.2.refs_0_.refs_2_), channel_id=1, source_target_pairs={{0,4},{4,0},{8,12},{12,8},{16,20},{20,16},{24,28},{28,24},{32,36},... | collective-permute-start | bytes 5505032 | tf_op jit(solution)/shard_map/ppermute | solution.py:218
  213.7 50.4 %collective-permute-start.8 = (bf16[64,8,1792]{2,1,0:T(8,128)(2,1)}, bf16[64,8,1792]{2,1,0:T(8,128)(2,1)S(1)}, u32[]{:S(2)}, u32[]{:S(2)}) collective-permute-start(bf16[64,8,1792]{2,1,0:T(8,128)(2,1)} %slice.6), channel_id=1, source_target_pairs={{0,1},{1,0},{2,3},{3,2},{4,5},{5,4},{6,7},{7,6},{8,9},{9,8},{10,11... | collective-permute-start | bytes 5505032 | tf_op jit(solution)/shard_map/ppermute | solution.py:221
  213.7 50.4 %collective-permute-start.9 = (bf16[64,8,1792]{2,1,0:T(8,128)(2,1)}, bf16[64,8,1792]{2,1,0:T(8,128)(2,1)S(1)}, u32[]{:S(2)}, u32[]{:S(2)}) collective-permute-start(bf16[64,8,1792]{2,1,0:T(8,128)(2,1)} %slice.7), channel_id=1, source_target_pairs={{0,3},{1,2},{2,1},{3,0},{4,7},{5,6},{6,5},{7,4},{8,11},{9,10},{10,... | collective-permute-start | bytes 5505032 | tf_op jit(solution)/shard_map/ppermute | solution.py:221
  216.1 14.9 %collective-permute-start.1 = (bf16[1,88,1408]{2,1,0:T(8,128)(2,1)S(1)}, bf16[1,88,1408]{2,1,0:T(8,128)(2,1)S(1)}, u32[]{:S(2)}, u32[]{:S(2)}) collective-permute-start(bf16[1,88,1408]{2,1,0:T(8,128)(2,1)S(1)} %get-tuple-element.32), channel_id=1, source_target_pairs={{64,0},{65,1},{66,2},{67,3},{68,128},{69,129},{70,130},{71,131},{7... | collective-permute-start | bytes 743432 | tf_op jit(solution)/shard_map/ppermute | solution.py:169
  216.1 15.1 %collective-permute-start.2 = (bf16[1,88,1408]{2,1,0:T(8,128)(2,1)S(1)}, bf16[1,88,1408]{2,1,0:T(8,128)(2,1)S(1)}, u32[]{:S(2)}, u32[]{:S(2)}) collective-permute-start(bf16[1,88,1408]{2,1,0:T(8,128)(2,1)S(1)} %get-tuple-element.33), channel_id=1, source_target_pairs={{64,128},{65,129},{66,130},{67,131},{68,0},{69,1},{70,2},{71,3},{7... | collective-permute-start | bytes 743432 | tf_op jit(solution)/shard_map/ppermute | solution.py:169
  231.0 16.0 %collective-permute-start.10 = (bf16[1,88,1408]{2,1,0:T(8,128)(2,1)S(1)}, bf16[1,88,1408]{2,1,0:T(8,128)(2,1)S(1)}, u32[]{:S(2)}, u32[]{:S(2)}) collective-permute-start(bf16[1,88,1408]{2,1,0:T(8,128)(2,1)S(1)} %get-tuple-element.43), channel_id=1, source_target_pairs={{64,0},{65,1},{66,2},{67,3},{68,131},{69,130},{70,129},{71,128},{7... | collective-permute-start | bytes 743432 | tf_op jit(solution)/shard_map/ppermute | solution.py:169
  231.2 15.8 %copy-start.10 = (bf16[1,88,1408]{2,1,0:T(8,128)(2,1)S(1)}, bf16[1,88,1408]{2,1,0:T(8,128)(2,1)}, u32[]{:S(2)}) copy-start(bf16[1,88,1408]{2,1,0:T(8,128)(2,1)} %copy-done.9) | copy-start | bytes 743428
  231.2 19.4 %collective-permute-start.11 = (bf16[1,88,1408]{2,1,0:T(8,128)(2,1)}, bf16[1,88,1408]{2,1,0:T(8,128)(2,1)S(1)}, u32[]{:S(2)}, u32[]{:S(2)}) collective-permute-start(bf16[1,88,1408]{2,1,0:T(8,128)(2,1)} %get-tuple-element.44), channel_id=1, source_target_pairs={{64,131},{65,130},{66,129},{67,128},{68,0},{69,1},{70,2},{71,3},{7... | collective-permute-start | bytes 743432 | tf_op jit(solution)/shard_map/ppermute | solution.py:169
  234.8 12.0 %copy-start = (bf16[64,8,1792]{2,1,0:T(8,128)(2,1)}, bf16[64,8,1792]{2,1,0:T(8,128)(2,1)S(1)}, u32[]{:S(2)}) copy-start(bf16[64,8,1792]{2,1,0:T(8,128)(2,1)S(1)} %collective-permute-done.7.refs_1_.refs_3_) | copy-start | bytes 5505028
  234.8 15.8 %collective-permute-start.5 = (bf16[1,88,1408]{2,1,0:T(8,128)(2,1)}, bf16[1,88,1408]{2,1,0:T(8,128)(2,1)S(1)}, u32[]{:S(2)}, u32[]{:S(2)}) collective-permute-start(bf16[1,88,1408]{2,1,0:T(8,128)(2,1)} %get-tuple-element.37), channel_id=1, source_target_pairs={{64,0},{65,1},{66,2},{67,3},{68,129},{69,128},{70,131},{71,130},{7... | collective-permute-start | bytes 743432 | tf_op jit(solution)/shard_map/ppermute | solution.py:169
  247.0 17.1 %collective-permute-start.6 = (bf16[1,88,1408]{2,1,0:T(8,128)(2,1)S(1)}, bf16[1,88,1408]{2,1,0:T(8,128)(2,1)S(1)}, u32[]{:S(2)}, u32[]{:S(2)}) collective-permute-start(bf16[1,88,1408]{2,1,0:T(8,128)(2,1)S(1)} %copy-done.10), channel_id=1, source_target_pairs={{64,129},{65,128},{66,131},{67,130},{68,0},{69,1},{70,2},{71,3},{7... | collective-permute-start | bytes 743432 | tf_op jit(solution)/shard_map/ppermute | solution.py:169
  250.6 16.8 %collective-permute-start.12 = (bf16[1,88,1408]{2,1,0:T(8,128)(2,1)S(1)}, bf16[1,88,1408]{2,1,0:T(8,128)(2,1)S(1)}, u32[]{:S(2)}, u32[]{:S(2)}) collective-permute-start(bf16[1,88,1408]{2,1,0:T(8,128)(2,1)S(1)} %get-tuple-element.45), channel_id=1, source_target_pairs={{64,0},{65,1},{66,2},{67,3},{68,128},{69,129},{70,130},{71,131},{7... | collective-permute-start | bytes 743432 | tf_op jit(solution)/shard_map/ppermute | solution.py:169
  250.6 17.9 %collective-permute-start.13 = (bf16[1,88,1408]{2,1,0:T(8,128)(2,1)S(1)}, bf16[1,88,1408]{2,1,0:T(8,128)(2,1)S(1)}, u32[]{:S(2)}, u32[]{:S(2)}) collective-permute-start(bf16[1,88,1408]{2,1,0:T(8,128)(2,1)S(1)} %get-tuple-element.46), channel_id=1, source_target_pairs={{64,128},{65,129},{66,130},{67,131},{68,0},{69,1},{70,2},{71,3},{7... | collective-permute-start | bytes 743432 | tf_op jit(solution)/shard_map/ppermute | solution.py:169
  264.1 25.1 %collective-permute-start.16 = (bf16[1,88,1408]{2,1,0:T(8,128)(2,1)S(1)}, bf16[1,88,1408]{2,1,0:T(8,128)(2,1)S(1)}, u32[]{:S(2)}, u32[]{:S(2)}) collective-permute-start(bf16[1,88,1408]{2,1,0:T(8,128)(2,1)S(1)} %get-tuple-element.51), channel_id=1, source_target_pairs={{64,0},{65,1},{66,2},{67,3},{68,129},{69,128},{70,131},{71,130},{7... | collective-permute-start | bytes 743432 | tf_op jit(solution)/shard_map/ppermute | solution.py:169
  264.1 4.4 %copy-start.11 = (bf16[64,8,1792]{2,1,0:T(8,128)(2,1)}, bf16[64,8,1792]{2,1,0:T(8,128)(2,1)S(1)}, u32[]{:S(2)}) copy-start(bf16[64,8,1792]{2,1,0:T(8,128)(2,1)S(1)} %collective-permute-done.8.refs_4_) | copy-start | bytes 5505028
  264.1 4.4 %copy-start.12 = (bf16[64,8,1792]{2,1,0:T(8,128)(2,1)}, bf16[64,8,1792]{2,1,0:T(8,128)(2,1)S(1)}, u32[]{:S(2)}) copy-start(bf16[64,8,1792]{2,1,0:T(8,128)(2,1)S(1)} %collective-permute-done.9.refs_5_) | copy-start | bytes 5505028
  267.4 0.7 copy-start.3
  268.5 0.7 copy-start.5
  278.4 45.5 %collective-permute-start.14 = (bf16[2,88,1408]{2,1,0:T(8,128)(2,1)}, bf16[2,88,1408]{2,1,0:T(8,128)(2,1)S(1)}, u32[]{:S(2)}, u32[]{:S(2)}) collective-permute-start(bf16[2,88,1408]{2,1,0:T(8,128)(2,1)} %get-tuple-element.49), channel_id=1, source_target_pairs={{64,0},{65,1},{66,2},{67,3},{68,130},{69,131},{70,128},{71,129},{7... | collective-permute-start | bytes 1486856 | tf_op jit(solution)/shard_map/ppermute | solution.py:169
  279.5 44.5 %collective-permute-start.15 = (bf16[2,88,1408]{2,1,0:T(8,128)(2,1)}, bf16[2,88,1408]{2,1,0:T(8,128)(2,1)S(1)}, u32[]{:S(2)}, u32[]{:S(2)}) collective-permute-start(bf16[2,88,1408]{2,1,0:T(8,128)(2,1)} %get-tuple-element.50), channel_id=1, source_target_pairs={{64,130},{65,131},{66,128},{67,129},{68,0},{69,1},{70,2},{71,3},{7... | collective-permute-start | bytes 1486856 | tf_op jit(solution)/shard_map/ppermute | solution.py:169
  286.3 31.5 %collective-permute-start.17 = (bf16[1,88,1408]{2,1,0:T(8,128)(2,1)}, bf16[1,88,1408]{2,1,0:T(8,128)(2,1)}, u32[]{:S(2)}, u32[]{:S(2)}) collective-permute-start(bf16[1,88,1408]{2,1,0:T(8,128)(2,1)} %get-tuple-element.52), channel_id=1, source_target_pairs={{64,129},{65,128},{66,131},{67,130},{68,0},{69,1},{70,2},{71,3},{7... | collective-permute-start | bytes 743432 | tf_op jit(solution)/shard_map/ppermute | solution.py:169
  289.2 28.6 %collective-permute-start.18 = (bf16[1,88,1408]{2,1,0:T(8,128)(2,1)}, bf16[1,88,1408]{2,1,0:T(8,128)(2,1)}, u32[]{:S(2)}, u32[]{:S(2)}) collective-permute-start(bf16[1,88,1408]{2,1,0:T(8,128)(2,1)} %get-tuple-element.53), channel_id=1, source_target_pairs={{64,0},{65,1},{66,2},{67,3},{68,131},{69,130},{70,129},{71,128},{7... | collective-permute-start | bytes 743432 | tf_op jit(solution)/shard_map/ppermute | solution.py:169
  289.2 0.7 copy-start.7
  289.9 34.1 %collective-permute-start.19 = (bf16[1,88,1408]{2,1,0:T(8,128)(2,1)}, bf16[1,88,1408]{2,1,0:T(8,128)(2,1)}, u32[]{:S(2)}, u32[]{:S(2)}) collective-permute-start(bf16[1,88,1408]{2,1,0:T(8,128)(2,1)} %get-tuple-element.54), channel_id=1, source_target_pairs={{64,131},{65,130},{66,129},{67,128},{68,0},{69,1},{70,2},{71,3},{7... | collective-permute-start | bytes 743432 | tf_op jit(solution)/shard_map/ppermute | solution.py:169
  324.0 0.9 copy-start.4
  324.9 0.9 copy-start.6
  325.9 0.9 copy-start.8

commit v4 on v3

--- a/solution.py
+++ b/solution.py
@@ -56,12 +56,12 @@
     return cut + ([(slice(whole, quarter), slice(start, start + rest))] if rest else [])
 
 
-def pack_body(l_ref, x_ref, m_ref, *k_refs):
+def pack_body(l_ref, x_ref, m_ref, k_ref):
     quarter = l_ref.shape[1]
     spots, half = m_ref.shape[0], m_ref.shape[-1] // 2
     turned = []
     for ref in (l_ref, x_ref):
-        block = jnp.swapaxes(jnp.swapaxes(ref[...].astype(jnp.float32), 1, 2), 0, 1)
+        block = jnp.swapaxes(jnp.swapaxes(ref[...], 1, 2).astype(jnp.float32), 0, 1)
         turned.append(block.astype(jnp.bfloat16).reshape(2, spots, 2, SUB, quarter))
     step = pl.program_id(0)
     n_groups = half // quarter
@@ -71,7 +71,7 @@
         def _():
             for r in range(2):
                 places = [(turned[1 - r][1, :, r], m_ref, 0), (turned[r][1, :, r], m_ref, half)]
-                places += [(turned[r][0, :, i], k_ref, 0) for i, k_ref in enumerate(k_refs)]
+                places += [(turned[r][0, :, i], k_ref, i * half) for i in range(2)]
                 for block, ref, start in places:
                     for of, to in pieces(quarter, n_groups, at):
                         ref[:, r, :, start + to.start : start + to.stop] = block[:, :, of]
@@ -81,7 +81,7 @@
     rows, quarter, orbitals = chol.shape
     spots, groups = orbitals // 4, rows // SUB
     lanes = ceil_lanes(groups * quarter)
-    shapes = [(spots, 2, SUB, wide) for wide in (2 * lanes, lanes, lanes)]
+    shapes = [(spots, 2, SUB, wide) for wide in (2 * lanes, 2 * lanes)]
     out = pl.pallas_call(
         pack_body,
         grid=(groups,),
@@ -147,7 +147,7 @@
 def tiles(name, quarter, core, lefts, rights, messages):
     ops = [op if isinstance(op, tuple) else (op, 0) for pair in (*lefts, *rights) for op in pair]
     arrays = [array for array, _ in ops]
-    width, _, lanes = arrays[0].shape
+    width, lanes = arrays[0].shape[0], arrays[0].shape[-1] // 2
     groups = lanes // quarter
     shapes = [(len(message), quarter // 4, 4 * quarter) for message in messages] * 2
     out = pl.pallas_call(
@@ -170,7 +170,7 @@
     ]
 
 
-def home_body(index, where_ref, pairs_ref, mask_ref, *refs):
+def home_body(where_ref, pairs_ref, mask_ref, *refs):
     arrived, out_ref, held = refs[:-2], refs[-2], refs[-1]
     is_k, g = where_ref[0], where_ref[1]
     u, v = pl.program_id(0), pl.program_id(1)
@@ -184,8 +184,8 @@
             @pl.when((use == at) & (i == orbital))
             def _():
                 for bits in range(4):
-                    ref = arrived[2 * (4 * orbital + bits) + at]
-                    parts = [ref[index[bits, orbital], :, n * quarter : (n + 1) * quarter].astype(jnp.float32) for n in range(4)]
+                    ref = arrived[2 * bits + at]
+                    parts = [ref[orbital, :, n * quarter : (n + 1) * quarter].astype(jnp.float32) for n in range(4)]
                     held[bits] = jnp.concatenate(parts, axis=0).astype(jnp.bfloat16)
 
     for q in range(4):
@@ -193,11 +193,11 @@
         out_ref[0, 0, :, lanes] = held[q ^ g] * (mask_ref[:, lanes] * scale)
 
 
-def home(index, where, pairs, mask, arrays):
+def home(where, pairs, mask, arrays):
     quarter, whole = mask.shape
     full = [pl.BlockSpec(a.shape, lambda u, v, k=a.ndim: (0,) * k) for a in (mask, *arrays)]
     return pl.pallas_call(
-        functools.partial(home_body, index),
+        home_body,
         grid=(2, 2),
         in_specs=[pl.BlockSpec(memory_space=pltpu.SMEM)] * 2 + full,
         out_specs=pl.BlockSpec((1, 1, quarter, whole), lambda u, v: (u, v, 0, 0)),
@@ -226,38 +226,30 @@
     def centre(part):
         return lax.all_to_all(part, "occ", 0, 0, axis_index_groups=order, tiled=True)
 
-    (m, k0, k1), lanes = pack(*[jnp.transpose(a, (0, 2, 1)) for a in (chol, dressed)])
-    m, k0, k1 = centre(m), centre(k0), centre(k1)
+    (m, k), lanes = pack(*[jnp.transpose(a, (0, 2, 1)) for a in (chol, dressed)])
+    m, k = centre(m), centre(k)
 
     m_1, m_3 = across(m, 1), across(m, 3)
-    k0 = (k0, to_core(k0))
-    ms = {0: ((m, 0), (m, 1))}
+    m_2 = across(m_3[:, :, :lanes], 1), across(m_1[:, :, lanes:], 3)
+    k_core = to_core(k)
+    ks = [((k, i), (k_core, i)) for i in range(2)]
+    ms = {q: ((array, 0), (array, 1)) for q, array in ((0, m), (1, m_1), (3, m_3))}
     got = {}
 
-    def compute(name, ks, spots):
-        messages = [[(left, right) for left in range(len(ks))] for right in range(len(spots))]
+    def compute(name, spots):
+        messages = [[(left, right) for left in range(2)] for right in range(len(spots))]
         return tiles(name, quarter, core, ks, [ms[q] for q in spots], messages)
 
-    first = compute("first", [k0], [0])
-    got[0, 0] = send(first[0], 0, 0)
-    m_1, m_3 = lax.optimization_barrier((m_1, m_3, *first[0]))[:2]
+    (first,) = compute("first", [0])
+    got[0] = send(first, 0, 0)
+    m_1, m_3 = lax.optimization_barrier((m_1, m_3, *first))[:2]
     ms |= {1: ((m_1, 0), (m_1, 1)), 3: ((m_3, 0), (m_3, 1))}
-    m_2 = m_3[:, :, :lanes], m_1[:, :, lanes:]
-    k0_own, *m_2 = lax.optimization_barrier((k0[0], *m_2))
-    m_2 = across(m_2[0], 1), across(m_2[1], 3)
-    k0 = (k0_own, k0[1])
-    second = compute("second", [k0], [1, 3])
-    got[1, 0], got[3, 0] = send(second[0], 0, 1), send(second[1], 0, 3)
-    k1 = after(k1, *second[0])
-    k1 = (k1, to_core(k1))
-    third = compute("third", [k1], [0, 1, 3])
-    for q, message in zip((0, 1, 3), third):
-        got[q, 1] = send(message, 0, q)
-    ms[2] = lax.optimization_barrier((*m_2, *got[0, 0], *got[1, 0], *got[3, 0], *got[0, 1]))[:2]
-    fourth = compute("fourth", [k0, k1], [2])
-    got[2, 0] = got[2, 1] = send(fourth[0], 0, 2)
-    arrived = [a for i in range(2) for q in range(4) for a in got[q, i]]
-    index = {(q, i): i if q == 2 else 0 for q in range(4) for i in range(2)}
+    second = compute("second", [1, 3])
+    got[1], got[3] = send(second[0], 0, 1), send(second[1], 0, 3)
+    ms[2] = lax.optimization_barrier((*m_2, *got[0], *second[0]))[:2]
+    (third,) = compute("third", [2])
+    got[2] = send(third, 0, 2)
+    arrived = [a for q in range(4) for a in got[q]]
 
     mirror = (occ + PLACES // 2) % PLACES
     pairs = lax.dynamic_slice(pair_mask, (occ * 2, mirror * 2), (2, 2))
@@ -265,7 +257,7 @@
     sym_rows = lax.dynamic_slice_in_dim(sym_mask, g * rows_per, rows_per, 0)
     mask = jnp.repeat(jnp.repeat(sym_rows.astype(jnp.bfloat16), SLAB, 0), SLAB, 1)
     where = jnp.stack([(occ < PLACES // 2).astype(jnp.int32), g.astype(jnp.int32)])
-    return home(index, where, pairs, mask, arrived)
+    return home(where, pairs, mask, arrived)
 
 
 def solution(mesh):

time: 335 us -> 318 us (0.949)
  waiting for transfers between devices: 121 us -> 111 us
  local copies, waits for them, and re-layouts: 15 us -> 11.4 us
    all_to_all x2 -> x1, waiting for transfers between devices: 40.9 us -> 80.5 us  [centre(): lax.all_to_all(part, 'occ', 0, 0, axis_index_groups=order, tiled=True)]
    ppermute x14 -> x8, waiting for transfers between devices: 53.5 us -> 28 us  [send(): lax.ppermute(pair[at], ('occ', 'vir'), home_route(at == 0, k_bits, m_bits))]
    ppermute x4, waiting for transfers between devices: 22.9 us -> 2.24 us  [across(): return lax.ppermute(part, 'vir', x_route(bits))]
    all_to_all x2 -> x1, starting transfers between devices: 14.1 us -> 7.18 us  [centre(): lax.all_to_all(part, 'occ', 0, 0, axis_index_groups=order, tiled=True)]
    ppermute x14 -> x8, starting transfers between devices: 26.6 us -> 30.4 us  [send(): lax.ppermute(pair[at], ('occ', 'vir'), home_route(at == 0, k_bits, m_bits))]
    ppermute x2 -> x1, waiting for transfers between devices: 3.77 us -> 0.01 us  [to_core(): return lax.ppermute(part, 'occ', core_route())]
    pallas_call x4 -> x3, Pallas kernels: 35.8 us -> 32.1 us  [tiles(): pl.pallas_call(functools.partial(tiles_body, len(lefts), len(rights), mes...]
    unnamed x26 -> x2, local copies, waits for them, and re-layouts: 5.67 us -> 2.02 us
  transfers between devices with their start and end apart: 22 -> 14, of which waited for: 12 -> 6; matrix products, arithmetic and copies ran while one was open for 3% -> 3% of each run, Pallas kernels for 11% -> 10%
where the time goes in v4:
time: 318 us; the launch traced here: 314 us
  waiting for transfers between devices  111 us (35%)
  blocking collectives  97 us (31%)
  Pallas kernels  49.4 us (16%)
  starting transfers between devices  44.3 us (14%)
  local copies, waits for them, and re-layouts  11.4 us (4%)
    all_to_all x1, blocking collectives, centre(): lax.all_to_all(part, 'occ', 0, 0, axis_index_groups=order, tiled=True)  97 us
    all_to_all x1, waiting for transfers between devices, centre(): lax.all_to_all(part, 'occ', 0, 0, axis_index_groups=order, tiled=True)  80.5 us
    pallas_call x3, Pallas kernels, tiles(): pl.pallas_call(functools.partial(tiles_body, len(lefts), len(rights), mes...  32.1 us
    ppermute x8, starting transfers between devices, send(): lax.ppermute(pair[at], ('occ', 'vir'), home_route(at == 0, k_bits, m_bits))  30.4 us
    ppermute x8, waiting for transfers between devices, send(): lax.ppermute(pair[at], ('occ', 'vir'), home_route(at == 0, k_bits, m_bits))  28 us
    pallas_call x1, Pallas kernels, pack(): pl.pallas_call(pack_body, grid=(groups,), in_specs=[pl.BlockSpec((SUB, qu...  10.9 us
    all_to_all x1, starting transfers between devices, centre(): lax.all_to_all(part, 'occ', 0, 0, axis_index_groups=order, tiled=True)  7.18 us
    ppermute x4, starting transfers between devices, across(): return lax.ppermute(part, 'vir', x_route(bits))  6.66 us
  transfers between devices with their start and end apart: 14, of which 6 were waited for; matrix products, arithmetic and copies ran while one was open for 3% of the time, Pallas kernels for 10%

profile of v4, /device:TPU:8, one launch (start us, length us, event | category | flops | bytes accessed | tf_op | source)
XLA Modules:
  0.0 313.7 jit_solution(8328556134661352950)
XLA Ops:
  0.0 0.0 copy-start
  0.0 2.0 copy-done
  2.0 10.9 %pack.1 = (bf16[32,2,8,3584]{3,2,1,0:T(8,128)(2,1)}, bf16[32,2,8,3584]{3,2,1,0:T(8,128)(2,1)}) custom-call(bf16[40,352,128]{2,1,0:T(8,128)(2,1)S(1)} %bitcast.9, bf16[40,352,128]{2,1,0:T(8,128)(2,1)} %bitcast.13), custom_call_target="tpu_custom_call" | custom-call | tf_op jit(solution)/shard_map/pack/pallas_call | solution.py:85
  12.9 97.0 %all_to_all.10.refs_4_.refs_5_ = bf16[64,8,3584]{2,1,0:T(8,128)(2,1)} all-to-all(bf16[64,8,3584]{2,1,0:T(8,128)(2,1)} %bitcast.12), channel_id=1, replica_groups={{64,68,192,196,72,76,200,204,80,84,208,212,88,92,216,220,96,100,224,228..., dimensions={0} | all-to-all | bytes 7340032 | tf_op jit(solution)/shard_map/all_to_all | solution.py:227
  109.9 7.2 %all-to-all-start = ((bf16[64,8,3584]{2,1,0:T(8,128)(2,1)}), bf16[64,8,3584]{2,1,0:T(8,128)(2,1)}, u32[]{:S(2)}, u32[]{:S(2)}) async-start(bf16[64,8,3584]{2,1,0:T(8,128)(2,1)} %bitcast.11), calls=%async_computation | async-start | bytes 7340032 | tf_op jit(solution)/shard_map/all_to_all | solution.py:227
  117.1 2.8 collective-permute-start.4
  119.9 0.2 collective-permute-start.3
  120.1 80.5 %all-to-all-done.refs_0_.refs_2_ = bf16[64,8,3584]{2,1,0:T(8,128)(2,1)} async-done(((bf16[64,8,3584]{2,1,0:T(8,128)(2,1)}), bf16[64,8,3584]{2,1,0:T(8,128)(2,1)}, u32[]{:S(2)}, u32[]{:S(2)}) %all-to-all-start) | async-done | bytes 3670048 | tf_op jit(solution)/shard_map/all_to_all | solution.py:227
  200.7 0.0 collective-permute-start
  200.7 0.0 collective-permute-done.4.refs_6_.refs_7_
  200.7 2.8 slice.8
  203.5 1.5 collective-permute-start.7
  205.0 0.0 collective-permute-done.3.refs_4_.refs_5_
  205.0 2.9 slice.9
  207.9 2.1 collective-permute-start.8
  210.0 0.0 collective-permute-done.refs_1_.refs_3_
  210.0 8.5 %first.1 = (bf16[2,88,1408]{2,1,0:T(8,128)(2,1)S(1)}, bf16[2,88,1408]{2,1,0:T(8,128)(2,1)S(1)}) custom-call(s32[1]{0:T(128)} %bitcast.4.core_ref, bf16[64,8,3584]{2,1,0:T(8,128)(2,1)} %all-to-all-done.refs_0_.refs_2_, bf16[64,8,3584]{2,1,0:T(8,128)(2,1)} %collective-permute-done.refs_1_.refs_3_, bf16[64,8,3584]{2,1,0:T(8,128)(2,1)} %all-to-all-done.refs_0_.refs_2_, ...), custom_call_target="tpu_custom_call" | custom-call | tf_op jit(solution)/shard_map/first/pallas_call | solution.py:153
  218.5 0.1 collective-permute-start.1
  218.6 1.0 collective-permute-start.2
  219.6 14.3 %second.1 = (bf16[2,88,1408]{2,1,0:T(8,128)(2,1)}, bf16[2,88,1408]{2,1,0:T(8,128)(2,1)S(1)}, bf16[2,88,1408]{2,1,0:T(8,128)(2,1)}, bf16[2,88,1408]{2,1,0:T(8,128)(2,1)}) custom-call(s32[1]{0:T(128)} %bitcast.4.core_ref, bf16[64,8,3584]{2,1,0:T(8,128)(2,1)} %all-to-all-done.refs_0_.refs_2_, bf16[64,8,3584]{2,1,0:T(8,128)(2,1)} %collective-permute-done.refs_1_.refs_3_, ...), custom_call_target="tpu_custom_call" | custom-call | tf_op jit(solution)/shard_map/second/pallas_call | solution.py:153
  234.0 1.9 collective-permute-start.11
  235.8 7.6 %collective-permute-done.1.refs_0_ = bf16[2,88,1408]{2,1,0:T(8,128)(2,1)S(1)} collective-permute-done((bf16[2,88,1408]{2,1,0:T(8,128)(2,1)S(1)}, bf16[2,88,1408]{2,1,0:T(8,128)(2,1)S(1)}, u32[]{:S(2)}, u32[]{:S(2)}) %collective-permute-start.1) | collective-permute-done | bytes 495648 | tf_op jit(solution)/shard_map/ppermute | solution.py:169
  243.4 1.8 collective-permute-start.12
  245.2 0.0 collective-permute-done.2.refs_1_
  245.2 0.9 collective-permute-start.5
  246.0 0.1 collective-permute-done.7.refs_4_
  246.2 3.3 %collective-permute-start.6 = (bf16[2,88,1408]{2,1,0:T(8,128)(2,1)}, bf16[2,88,1408]{2,1,0:T(8,128)(2,1)}, u32[]{:S(2)}, u32[]{:S(2)}) collective-permute-start(bf16[2,88,1408]{2,1,0:T(8,128)(2,1)} %get-tuple-element.26), channel_id=1, source_target_pairs={{64,129},{65,128},{66,131},{67,130},{68,0},{69,1},{70,2},{71,3},{7... | collective-permute-start | bytes 1486856 | tf_op jit(solution)/shard_map/ppermute | solution.py:169
  249.4 2.1 collective-permute-done.8.refs_5_
  251.6 9.2 %third.1 = (bf16[2,88,1408]{2,1,0:T(8,128)(2,1)}, bf16[2,88,1408]{2,1,0:T(8,128)(2,1)}) custom-call(s32[1]{0:T(128)} %bitcast.4.core_ref, bf16[64,8,3584]{2,1,0:T(8,128)(2,1)} %all-to-all-done.refs_0_.refs_2_, bf16[64,8,3584]{2,1,0:T(8,128)(2,1)} %collective-permute-done.refs_1_.refs_3_, bf16[64,8,3584]{2,1,0:T(8,128)(2,1)} %all-to-all-done.refs_0_.refs_2_, ...), custom_call_target="tpu_custom_call" | custom-call | tf_op jit(solution)/shard_map/third/pallas_call | solution.py:153
  260.8 21.5 %collective-permute-start.10 = (bf16[2,88,1408]{2,1,0:T(8,128)(2,1)}, bf16[2,88,1408]{2,1,0:T(8,128)(2,1)S(1)}, u32[]{:S(2)}, u32[]{:S(2)}) collective-permute-start(bf16[2,88,1408]{2,1,0:T(8,128)(2,1)} %get-tuple-element.30), channel_id=1, source_target_pairs={{64,130},{65,131},{66,128},{67,129},{68,0},{69,1},{70,2},{71,3},{7... | collective-permute-start | bytes 1486856 | tf_op jit(solution)/shard_map/ppermute | solution.py:169
  282.3 0.0 collective-permute-done.11.refs_6_
  282.3 0.0 collective-permute-start.9
  282.3 0.7 dynamic-slice_convert_fusion
  283.1 0.1 copy.7
  283.2 1.1 broadcast_in_dim.7
  284.3 1.7 copy.8.mask_ref
  285.9 0.8 dynamic_slice.6.pairs_ref
  286.7 0.1 pad_add_fusion.where_ref
  286.8 0.0 collective-permute-done.12.refs_7_
  286.8 0.0 collective-permute-done.5.refs_2_
  286.8 0.0 collective-permute-done.6.refs_3_
  286.8 19.5 %collective-permute-done.10.refs_5_ = bf16[2,88,1408]{2,1,0:T(8,128)(2,1)S(1)} collective-permute-done((bf16[2,88,1408]{2,1,0:T(8,128)(2,1)}, bf16[2,88,1408]{2,1,0:T(8,128)(2,1)S(1)}, u32[]{:S(2)}, u32[]{:S(2)}) %collective-permute-start.10) | collective-permute-done | bytes 495648 | tf_op jit(solution)/shard_map/ppermute | solution.py:169
  306.4 0.9 collective-permute-done.9.refs_4_
  307.3 6.5 %home.1 = bf16[2,2,352,1408]{3,2,1,0:T(8,128)(2,1)} custom-call(s32[2]{0:T(128)S(1)} %pad_add_fusion.where_ref, s32[2,2]{1,0:T(2,128)S(1)} %dynamic_slice.6.pairs_ref, bf16[352,1408]{1,0:T(8,128)(2,1)S(1)} %copy.8.mask_ref, bf16[2,88,1408]{2,1,0:T(8,128)(2,1)S(1)} %collective-permute-done.1.refs_0_, bf16[2,88,1408]{2,1,0:T(8,128)(2,1)S(1)} %collective-permute-done.2.refs_1_, ...), custom_call_target="tpu_custom_call" | custom-call | tf_op jit(solution)/shard_map/home/pallas_call | solution.py:199
  (1 shorter events, 0.0 us)
Async XLA Ops:
  0.0 2.0 copy-start
  109.9 90.8 %all-to-all-start = ((bf16[64,8,3584]{2,1,0:T(8,128)(2,1)}), bf16[64,8,3584]{2,1,0:T(8,128)(2,1)}, u32[]{:S(2)}, u32[]{:S(2)}) async-start(bf16[64,8,3584]{2,1,0:T(8,128)(2,1)} %bitcast.11), calls=%async_computation | async-start | bytes 7340032 | tf_op jit(solution)/shard_map/all_to_all | solution.py:227
  117.1 83.6 %collective-permute-start.4 = (bf16[64,8,3584]{2,1,0:T(8,128)(2,1)}, bf16[64,8,3584]{2,1,0:T(8,128)(2,1)}, u32[]{:S(2)}, u32[]{:S(2)}) collective-permute-start(bf16[64,8,3584]{2,1,0:T(8,128)(2,1)} %all_to_all.10.refs_4_.refs_5_), channel_id=1, source_target_pairs={{0,3},{1,2},{2,1},{3,0},{4,7},{5,6},{6,5},{7,4},{8,11},{9,10},{10,... | collective-permute-start | bytes 11010056 | tf_op jit(solution)/shard_map/ppermute | solution.py:221
  119.9 85.1 %collective-permute-start.3 = (bf16[64,8,3584]{2,1,0:T(8,128)(2,1)}, bf16[64,8,3584]{2,1,0:T(8,128)(2,1)}, u32[]{:S(2)}, u32[]{:S(2)}) collective-permute-start(bf16[64,8,3584]{2,1,0:T(8,128)(2,1)} %all_to_all.10.refs_4_.refs_5_), channel_id=1, source_target_pairs={{0,1},{1,0},{2,3},{3,2},{4,5},{5,4},{6,7},{7,6},{8,9},{9,8},{10,11... | collective-permute-start | bytes 11010056 | tf_op jit(solution)/shard_map/ppermute | solution.py:221
  200.7 9.3 %collective-permute-start = (bf16[64,8,3584]{2,1,0:T(8,128)(2,1)}, bf16[64,8,3584]{2,1,0:T(8,128)(2,1)}, u32[]{:S(2)}, u32[]{:S(2)}) collective-permute-start(bf16[64,8,3584]{2,1,0:T(8,128)(2,1)} %all-to-all-done.refs_0_.refs_2_), channel_id=1, source_target_pairs={{0,4},{4,0},{8,12},{12,8},{16,20},{20,16},{24,28},{28,24},{32,36},... | collective-permute-start | bytes 11010056 | tf_op jit(solution)/shard_map/ppermute | solution.py:218
  203.5 42.6 %collective-permute-start.7 = (bf16[64,8,1792]{2,1,0:T(8,128)(2,1)}, bf16[64,8,1792]{2,1,0:T(8,128)(2,1)S(1)}, u32[]{:S(2)}, u32[]{:S(2)}) collective-permute-start(bf16[64,8,1792]{2,1,0:T(8,128)(2,1)} %slice.8), channel_id=1, source_target_pairs={{0,1},{1,0},{2,3},{3,2},{4,5},{5,4},{6,7},{7,6},{8,9},{9,8},{10,11... | collective-permute-start | bytes 5505032 | tf_op jit(solution)/shard_map/ppermute | solution.py:221
  207.9 43.7 %collective-permute-start.8 = (bf16[64,8,1792]{2,1,0:T(8,128)(2,1)}, bf16[64,8,1792]{2,1,0:T(8,128)(2,1)}, u32[]{:S(2)}, u32[]{:S(2)}) collective-permute-start(bf16[64,8,1792]{2,1,0:T(8,128)(2,1)} %slice.9), channel_id=1, source_target_pairs={{0,3},{1,2},{2,1},{3,0},{4,7},{5,6},{6,5},{7,4},{8,11},{9,10},{10,... | collective-permute-start | bytes 5505032 | tf_op jit(solution)/shard_map/ppermute | solution.py:221
  218.5 24.9 %collective-permute-start.1 = (bf16[2,88,1408]{2,1,0:T(8,128)(2,1)S(1)}, bf16[2,88,1408]{2,1,0:T(8,128)(2,1)S(1)}, u32[]{:S(2)}, u32[]{:S(2)}) collective-permute-start(bf16[2,88,1408]{2,1,0:T(8,128)(2,1)S(1)} %get-tuple-element.21), channel_id=1, source_target_pairs={{64,0},{65,1},{66,2},{67,3},{68,128},{69,129},{70,130},{71,131},{7... | collective-permute-start | bytes 1486856 | tf_op jit(solution)/shard_map/ppermute | solution.py:169
  218.6 26.6 %collective-permute-start.2 = (bf16[2,88,1408]{2,1,0:T(8,128)(2,1)S(1)}, bf16[2,88,1408]{2,1,0:T(8,128)(2,1)S(1)}, u32[]{:S(2)}, u32[]{:S(2)}) collective-permute-start(bf16[2,88,1408]{2,1,0:T(8,128)(2,1)S(1)} %get-tuple-element.22), channel_id=1, source_target_pairs={{64,128},{65,129},{66,130},{67,131},{68,0},{69,1},{70,2},{71,3},{7... | collective-permute-start | bytes 1486856 | tf_op jit(solution)/shard_map/ppermute | solution.py:169
  234.0 48.3 %collective-permute-start.11 = (bf16[2,88,1408]{2,1,0:T(8,128)(2,1)S(1)}, bf16[2,88,1408]{2,1,0:T(8,128)(2,1)S(1)}, u32[]{:S(2)}, u32[]{:S(2)}) collective-permute-start(bf16[2,88,1408]{2,1,0:T(8,128)(2,1)S(1)} %get-tuple-element.31), channel_id=1, source_target_pairs={{64,0},{65,1},{66,2},{67,3},{68,131},{69,130},{70,129},{71,128},{7... | collective-permute-start | bytes 1486856 | tf_op jit(solution)/shard_map/ppermute | solution.py:169
  243.4 43.4 %collective-permute-start.12 = (bf16[2,88,1408]{2,1,0:T(8,128)(2,1)}, bf16[2,88,1408]{2,1,0:T(8,128)(2,1)}, u32[]{:S(2)}, u32[]{:S(2)}) collective-permute-start(bf16[2,88,1408]{2,1,0:T(8,128)(2,1)} %get-tuple-element.32), channel_id=1, source_target_pairs={{64,131},{65,130},{66,129},{67,128},{68,0},{69,1},{70,2},{71,3},{7... | collective-permute-start | bytes 1486856 | tf_op jit(solution)/shard_map/ppermute | solution.py:169
  245.2 41.6 %collective-permute-start.5 = (bf16[2,88,1408]{2,1,0:T(8,128)(2,1)}, bf16[2,88,1408]{2,1,0:T(8,128)(2,1)}, u32[]{:S(2)}, u32[]{:S(2)}) collective-permute-start(bf16[2,88,1408]{2,1,0:T(8,128)(2,1)} %get-tuple-element.25), channel_id=1, source_target_pairs={{64,0},{65,1},{66,2},{67,3},{68,129},{69,128},{70,131},{71,130},{7... | collective-permute-start | bytes 1486856 | tf_op jit(solution)/shard_map/ppermute | solution.py:169
  246.2 40.6 %collective-permute-start.6 = (bf16[2,88,1408]{2,1,0:T(8,128)(2,1)}, bf16[2,88,1408]{2,1,0:T(8,128)(2,1)}, u32[]{:S(2)}, u32[]{:S(2)}) collective-permute-start(bf16[2,88,1408]{2,1,0:T(8,128)(2,1)} %get-tuple-element.26), channel_id=1, source_target_pairs={{64,129},{65,128},{66,131},{67,130},{68,0},{69,1},{70,2},{71,3},{7... | collective-permute-start | bytes 1486856 | tf_op jit(solution)/shard_map/ppermute | solution.py:169
  260.8 45.6 %collective-permute-start.10 = (bf16[2,88,1408]{2,1,0:T(8,128)(2,1)}, bf16[2,88,1408]{2,1,0:T(8,128)(2,1)S(1)}, u32[]{:S(2)}, u32[]{:S(2)}) collective-permute-start(bf16[2,88,1408]{2,1,0:T(8,128)(2,1)} %get-tuple-element.30), channel_id=1, source_target_pairs={{64,130},{65,131},{66,128},{67,129},{68,0},{69,1},{70,2},{71,3},{7... | collective-permute-start | bytes 1486856 | tf_op jit(solution)/shard_map/ppermute | solution.py:169
  282.3 25.0 %collective-permute-start.9 = (bf16[2,88,1408]{2,1,0:T(8,128)(2,1)}, bf16[2,88,1408]{2,1,0:T(8,128)(2,1)}, u32[]{:S(2)}, u32[]{:S(2)}) collective-permute-start(bf16[2,88,1408]{2,1,0:T(8,128)(2,1)} %get-tuple-element.29), channel_id=1, source_target_pairs={{64,0},{65,1},{66,2},{67,3},{68,130},{69,131},{70,128},{71,129},{7... | collective-permute-start | bytes 1486856 | tf_op jit(solution)/shard_map/ppermute | solution.py:169
